TPU v7x, 512 devices: a whole 4x8x8 slice. The times are simulated.
512 devices in a mesh: expert: 64 (over x, z, core), tensor: 8 (over y).
Axes of the slice: x: 4, y: 8, z: 8, core: 2. Of those that a mesh axis runs over, the one named last changes fastest.
Arguments:
- tokens: bfloat16 [8192, 2048], P('expert', 'tensor'), may hold values from -6 to 6
- cotangent: bfloat16 [8192, 2048], P('expert', 'tensor'), may hold values from -6 to 6
- route_ids: int32 [8192, 6], P('expert'), may hold values from 0 to 63, all different within a row
- route_weights: float32 [8192, 6], P('expert'), may hold values from 0.05 to 0.5
- shared_gate: bfloat16 [1408, 2048], P('tensor'), may hold values from -0.125 to 0.125
- shared_up: bfloat16 [1408, 2048], P('tensor'), may hold values from -0.125 to 0.125
- shared_down: bfloat16 [1408, 2048], P('tensor'), may hold values from -0.15625 to 0.15625
- expert_gate: bfloat16 [64, 1408, 2048], P('expert', 'tensor'), may hold values from -0.125 to 0.125
- expert_up: bfloat16 [64, 1408, 2048], P('expert', 'tensor'), may hold values from -0.125 to 0.125
- expert_down: bfloat16 [64, 1408, 2048], P('expert', 'tensor'), may hold values from -0.15625 to 0.15625
Outputs:
- layer_output: bfloat16 [8192, 2048], P('expert', 'tensor')
- input_grad: bfloat16 [8192, 2048], P('expert', 'tensor')
Inputs may be any that keep to these rules, and one draw needn't show every extreme that they name: `route_ids`: each row names 6 different experts.
All inputs are finite; a program needn't handle non-finite values.
Results may differ from a plain program's by a relative error of at most 0.0051.
Values may be sent and summed in bfloat16 or wider, within the bound.
A program may use at most 64 MiB of HBM per device.

v0:
```python
import jax
import jax.numpy as jnp
from jax import lax
from jax.sharding import PartitionSpec as P


def silu_parts(pre_act):
    sigmoid_value = jax.nn.sigmoid(pre_act)
    return (pre_act * sigmoid_value, sigmoid_value * (1.0 + pre_act * (1.0 - sigmoid_value)))


def on_device(
    tokens,
    cotangent,
    route_ids,
    route_weights,
    shared_gate,
    shared_up,
    shared_down,
    expert_gate,
    expert_up,
    expert_down,
):
    expert_count = lax.axis_size("expert")
    tok_rows, top_count = route_ids.shape
    local_experts = expert_gate.shape[0]
    all_experts = local_experts * expert_count
    capacity = tok_rows * top_count // (2 * all_experts)
    slot_total = all_experts * capacity
    flat_ids = route_ids.reshape(-1)
    one_hot = (flat_ids[:, None] == jnp.arange(all_experts, dtype=jnp.int32)[None, :]).astype(
        jnp.int32
    )
    rank_in = jnp.sum((jnp.cumsum(one_hot, axis=0) - one_hot) * one_hot, axis=1)
    kept_mask = rank_in < capacity
    slot_index = jnp.where(kept_mask, flat_ids * capacity + rank_in, slot_total)
    slot_match = jnp.arange(slot_total, dtype=jnp.int32)[:, None] == slot_index[None, :]
    dispatch = jnp.any(slot_match.reshape(slot_total, tok_rows, top_count), axis=2).astype(
        jnp.bfloat16
    )
    gate_flat = route_weights.reshape(-1)
    slot_gate = jnp.sum(jnp.where(slot_match, gate_flat[None, :], 0.0), axis=1)
    gate_dispatch = dispatch.astype(jnp.float32) * slot_gate[:, None]
    x_full, c_full = (
        lax.all_gather(tokens, "tensor", axis=1, tiled=True),
        lax.all_gather(cotangent, "tensor", axis=1, tiled=True),
    )
    x_slots = jnp.dot(dispatch, x_full, preferred_element_type=jnp.float32).astype(jnp.bfloat16)
    g_slots = (
        slot_gate[:, None] * jnp.dot(dispatch, c_full, preferred_element_type=jnp.float32)
    ).astype(jnp.bfloat16)
    x_recv, g_recv = (
        lax.all_to_all(x_slots, "expert", split_axis=0, concat_axis=0, tiled=True),
        lax.all_to_all(g_slots, "expert", split_axis=0, concat_axis=0, tiled=True),
    )

    def owner_layout(values):
        shaped = values.reshape(expert_count, local_experts, capacity, values.shape[-1])
        return shaped.transpose(1, 0, 2, 3).reshape(
            local_experts, expert_count * capacity, values.shape[-1]
        )

    def source_layout(values):
        shaped = values.reshape(local_experts, expert_count, capacity, values.shape[-1])
        return shaped.transpose(1, 0, 2, 3).reshape(slot_total, values.shape[-1])

    x_own = owner_layout(x_recv)
    g_own = owner_layout(g_recv)
    gate_pre = jnp.einsum("erd,efd->erf", x_own, expert_gate, preferred_element_type=jnp.float32)
    up_pre = jnp.einsum("erd,efd->erf", x_own, expert_up, preferred_element_type=jnp.float32)
    act_value, act_slope = silu_parts(gate_pre)
    hidden = (act_value * up_pre).astype(jnp.bfloat16)
    grad_hidden = jnp.einsum("erd,efd->erf", g_own, expert_down, preferred_element_type=jnp.float32)
    grad_gate = (grad_hidden * up_pre * act_slope).astype(jnp.bfloat16)
    grad_up = (grad_hidden * act_value).astype(jnp.bfloat16)
    value_part = source_layout(
        jnp.einsum("erf,efd->erd", hidden, expert_down, preferred_element_type=jnp.float32).astype(
            jnp.bfloat16
        )
    )
    grads_joined = jnp.concatenate((grad_gate, grad_up), axis=2)
    weights_joined = jnp.concatenate((expert_gate, expert_up), axis=1)
    input_term = jnp.einsum(
        "erf,efd->erd", grads_joined, weights_joined, preferred_element_type=jnp.float32
    )
    input_part = source_layout(input_term.astype(jnp.bfloat16))
    shared_gate_pre = jnp.einsum(
        "td,fd->tf", x_full, shared_gate, preferred_element_type=jnp.float32
    )
    shared_up_pre = jnp.einsum("td,fd->tf", x_full, shared_up, preferred_element_type=jnp.float32)
    shared_act, shared_slope = silu_parts(shared_gate_pre)
    shared_hidden = (shared_act * shared_up_pre).astype(jnp.bfloat16)
    shared_value = jnp.dot(shared_hidden, shared_down, preferred_element_type=jnp.float32)
    shared_grad_hidden = jnp.einsum(
        "td,fd->tf", c_full, shared_down, preferred_element_type=jnp.float32
    )
    shared_grad_gate = (shared_grad_hidden * shared_up_pre * shared_slope).astype(jnp.bfloat16)
    shared_grad_up = (shared_grad_hidden * shared_act).astype(jnp.bfloat16)
    shared_input = jnp.dot(shared_grad_gate, shared_gate, preferred_element_type=jnp.float32)
    shared_input = shared_input + jnp.dot(
        shared_grad_up, shared_up, preferred_element_type=jnp.float32
    )
    value_back, input_back = (
        lax.all_to_all(value_part, "expert", split_axis=0, concat_axis=0, tiled=True),
        lax.all_to_all(input_part, "expert", split_axis=0, concat_axis=0, tiled=True),
    )
    early_value = shared_value + jnp.einsum(
        "st,sd->td",
        gate_dispatch,
        value_back.astype(jnp.float32),
        precision=lax.Precision.HIGHEST,
        preferred_element_type=jnp.float32,
    )
    early_input = shared_input + jnp.einsum(
        "st,sd->td",
        dispatch,
        input_back,
        precision=lax.Precision.HIGHEST,
        preferred_element_type=jnp.float32,
    )
    value_total, input_total = (
        lax.psum_scatter(early_value, "tensor", scatter_dimension=1, tiled=True),
        lax.psum_scatter(early_input, "tensor", scatter_dimension=1, tiled=True),
    )
    return (value_total.astype(jnp.bfloat16), input_total.astype(jnp.bfloat16))


def solution(mesh):
    in_specs = (
        P("expert", "tensor"),
        P("expert", "tensor"),
        P("expert", None),
        P("expert", None),
        P("tensor", None),
        P("tensor", None),
        P("tensor", None),
        P("expert", "tensor", None),
        P("expert", "tensor", None),
        P("expert", "tensor", None),
    )
    out_specs = (P("expert", "tensor"), P("expert", "tensor"))
    return jax.shard_map(
        on_device, mesh=mesh, in_specs=in_specs, out_specs=out_specs, check_vma=False
    )
```

profile of v0, /device:TPU:6, one launch (start us, length us, event | category | flops | bytes accessed | tf_op | source)
XLA Modules:
  0.0 333.4 jit_solution(1822526318146382311)
XLA Ops:
  7.2 0.0 copy-start
  7.2 0.8 broadcast_multiply_fusion
  7.9 0.8 copy.19
  8.7 0.1 eq.46
  8.9 0.1 eq.50
  9.0 27.1 %all_gather.6 = bf16[128,2048]{1,0:T(8,128)(2,1)S(1)} all-gather(bf16[128,256]{1,0:T(8,128)(2,1)} %param.10), channel_id=1, replica_groups=mesh['expert'=64,'tensor'=8] {'tensor'}, dimensions={1}, use_global_device_ids=true | all-gather | bytes 589824 | tf_op jit(solution)/shard_map/all_gather | solution.py:45
  36.2 0.1 copy.23
  36.3 1.8 reduce-window.6
  38.1 0.3 slice_reduce_fusion
  38.4 0.1 fusion.15
  38.5 0.1 reduce_sum.21
  38.7 0.1 copy.24
  38.7 0.2 fusion.2
  38.9 0.6 convolution_convert_fusion.2
  39.5 1.6 all_to_all.32
  41.1 14.1 %all-to-all-start = ((bf16[64,6,2048]{2,1,0:T(8,128)(2,1)}), bf16[64,6,2048]{2,1,0:T(8,128)(2,1)S(1)}, u32[]{:S(2)}, u32[]{:S(2)}) async-start(bf16[64,6,2048]{2,1,0:T(8,128)(2,1)} %all_to_all.32), calls=%async_computation | async-start | bytes 4194304 | tf_op jit(solution)/shard_map/all_to_all | solution.py:53
  55.2 0.1 copy.25
  55.3 0.1 broadcast_in_dim.27
  55.5 0.2 select_reduce_fusion
  55.7 25.5 %all_gather.7 = bf16[128,2048]{1,0:T(8,128)(2,1)S(1)} all-gather(bf16[128,256]{1,0:T(8,128)(2,1)S(1)} %copy-done.14), channel_id=1, replica_groups=mesh['expert'=64,'tensor'=8] {'tensor'}, dimensions={1}, use_global_device_ids=true | all-gather | bytes 589824 | tf_op jit(solution)/shard_map/all_gather | solution.py:46
  81.2 0.8 copy-done.3
  82.0 1.7 multiply_convert_fusion
  83.8 3.7 %all_to_all.38 = bf16[64,6,2048]{2,1,0:T(8,128)(2,1)} reshape(bf16[384,2048]{1,0:T(8,128)(2,1)} %multiply_convert_fusion) | data formatting | bytes 3145728 | tf_op jit(solution)/shard_map/all_to_all | solution.py:54
  87.5 16.7 %all-to-all-done = bf16[64,6,2048]{2,1,0:T(8,128)(2,1)S(1)} async-done(((bf16[64,6,2048]{2,1,0:T(8,128)(2,1)}), bf16[64,6,2048]{2,1,0:T(8,128)(2,1)S(1)}, u32[]{:S(2)}, u32[]{:S(2)}) %all-to-all-start) | async-done | bytes 1572896 | tf_op jit(solution)/shard_map/all_to_all | solution.py:53
  104.2 1.3 copy-done.2
  105.5 8.3 %all-to-all-start.2 = ((bf16[64,6,2048]{2,1,0:T(8,128)(2,1)}), bf16[64,6,2048]{2,1,0:T(8,128)(2,1)}, u32[]{:S(2)}, u32[]{:S(2)}) async-start(bf16[64,6,2048]{2,1,0:T(8,128)(2,1)} %all_to_all.38), calls=%async_computation.3 | async-start | bytes 4194304 | tf_op jit(solution)/shard_map/all_to_all | solution.py:54
  113.8 2.6 all_to_all.34
  116.4 0.0 copy-start.12
  116.4 1.8 fusion.6
  118.3 0.7 fusion.8
  119.0 0.7 copy-done.9
  119.7 0.6 convolution_convert_fusion
  120.3 1.6 all_to_all.35
  121.9 40.8 %all-to-all-done.2 = bf16[64,6,2048]{2,1,0:T(8,128)(2,1)} async-done(((bf16[64,6,2048]{2,1,0:T(8,128)(2,1)}), bf16[64,6,2048]{2,1,0:T(8,128)(2,1)}, u32[]{:S(2)}, u32[]{:S(2)}) %all-to-all-start.2) | async-done | bytes 1572896 | tf_op jit(solution)/shard_map/all_to_all | solution.py:54
  162.7 8.1 %all-to-all-start.1 = ((bf16[64,6,2048]{2,1,0:T(8,128)(2,1)}), bf16[64,6,2048]{2,1,0:T(8,128)(2,1)S(1)}, u32[]{:S(2)}, u32[]{:S(2)}) async-start(bf16[64,6,2048]{2,1,0:T(8,128)(2,1)} %all_to_all.35), calls=%async_computation.1 | async-start | bytes 4194304 | tf_op jit(solution)/shard_map/all_to_all | solution.py:104
  170.8 3.7 %all_to_all.40 = bf16[384,2048]{1,0:T(8,128)(2,1)} reshape(bf16[64,6,2048]{2,1,0:T(8,128)(2,1)} %all-to-all-done.2) | data formatting | bytes 3145728 | tf_op jit(solution)/shard_map/all_to_all | solution.py:54
  174.5 2.3 fusion.20
  176.8 2.2 convolution_convert_fusion.1
  179.0 3.7 %all_to_all.41 = bf16[64,6,2048]{2,1,0:T(8,128)(2,1)} reshape(bf16[384,2048]{1,0:T(8,128)(2,1)} %convolution_convert_fusion.1) | data formatting | bytes 3145728 | tf_op jit(solution)/shard_map/all_to_all | solution.py:105
  182.7 37.0 %all-to-all-done.1 = bf16[64,6,2048]{2,1,0:T(8,128)(2,1)S(1)} async-done(((bf16[64,6,2048]{2,1,0:T(8,128)(2,1)}), bf16[64,6,2048]{2,1,0:T(8,128)(2,1)S(1)}, u32[]{:S(2)}, u32[]{:S(2)}) %all-to-all-start.1) | async-done | bytes 1572896 | tf_op jit(solution)/shard_map/all_to_all | solution.py:104
  219.7 1.3 copy-done.1
  221.0 8.1 %all-to-all-start.3 = ((bf16[64,6,2048]{2,1,0:T(8,128)(2,1)}), bf16[64,6,2048]{2,1,0:T(8,128)(2,1)S(1)}, u32[]{:S(2)}, u32[]{:S(2)}) async-start(bf16[64,6,2048]{2,1,0:T(8,128)(2,1)} %all_to_all.41), calls=%async_computation.4 | async-start | bytes 4194304 | tf_op jit(solution)/shard_map/all_to_all | solution.py:105
  229.2 0.2 reduce-scatter.3.cloned.1.call-start
  229.4 0.0 copy-start.5
  229.4 1.5 fusion.38
  230.9 1.5 fusion.37
  232.5 1.4 fusion.25
  233.8 3.7 %all_to_all.37 = bf16[384,2048]{1,0:T(8,128)(2,1)} reshape(bf16[64,6,2048]{2,1,0:T(8,128)(2,1)} %copy-done.1) | data formatting | bytes 3145728 | tf_op jit(solution)/shard_map/all_to_all | solution.py:104
  237.6 3.9 %convolution_add_fusion.2 = f32[128,2048]{1,0:T(8,128)} fusion(f32[128,2048]{1,0:T(8,128)} %fusion.25, bf16[384,2048]{1,0:T(8,128)(2,1)} %all_to_all.37, f32[384]{0:T(512)S(1)} %select_reduce_fusion, pred[384,128]{1,0:T(8,128)(4,1)S(1)} %fusion.2), kind=kOutput, calls=%fused_computation.6 | convolution fusion | flops 1208369152 | bytes 3720704 | tf_op jit(solution)/shard_map/st,sd->td/dot_general | solution.py:107
  241.4 0.0 reduce-scatter.3.cloned.1.call-update
  241.5 0.0 reduce-scatter.5.cloned.1.call-start
  241.5 0.0 copy-start.6
  241.5 0.0 copy-start.7
  241.5 1.6 fusion.39
  243.1 1.2 fusion.26
  244.4 1.3 convolution_add_fusion.1
  245.7 32.4 %all-to-all-done.3 = bf16[64,6,2048]{2,1,0:T(8,128)(2,1)S(1)} async-done(((bf16[64,6,2048]{2,1,0:T(8,128)(2,1)}), bf16[64,6,2048]{2,1,0:T(8,128)(2,1)S(1)}, u32[]{:S(2)}, u32[]{:S(2)}) %all-to-all-start.3) | async-done | bytes 1572896 | tf_op jit(solution)/shard_map/all_to_all | solution.py:105
  278.1 1.4 all_to_all.43
  279.5 3.2 convolution_add_fusion
  282.7 0.0 reduce-scatter.5.cloned.1.call-update
  282.7 0.0 reduce-scatter.3.cloned.1.call-done
  282.8 1.5 convert_element_type.67
  284.3 40.7 %reduce-scatter.5.cloned.1.call-done = f32[128,256]{1,0:T(8,128)} async-done(((f32[128,2048]{1,0:T(8,128)}), f32[128,256]{1,0:T(8,128)}) %reduce-scatter.5.cloned.1.call-update) | async-done | bytes 131088 | tf_op jit(solution)/shard_map/reduce_scatter | solution.py:123
  325.0 1.5 convert_element_type.76
  (27 shorter events, 0.1 us)
Async XLA Ops:
  7.2 112.5 %copy-start = (bf16[1,176,2048]{2,1,0:T(8,128)(2,1)S(1)}, bf16[1,176,2048]{2,1,0:T(8,128)(2,1)}, u32[]{:S(2)}) copy-start(bf16[1,176,2048]{2,1,0:T(8,128)(2,1)} %param.19) | copy-start | bytes 2162692
  41.1 14.2 %copy-start.15 = (f32[128,6]{0,1:T(8,128)S(1)}, f32[128,6]{0,1:T(8,128)}, u32[]{:S(2)}) copy-start(f32[128,6]{0,1:T(8,128)} %param.13) | copy-start | bytes 9220
  41.1 14.6 %copy-start.14 = (bf16[128,256]{1,0:T(8,128)(2,1)S(1)}, bf16[128,256]{1,0:T(8,128)(2,1)}, u32[]{:S(2)}) copy-start(bf16[128,256]{1,0:T(8,128)(2,1)} %param.11) | copy-start | bytes 196612
  41.1 63.1 %all-to-all-start = ((bf16[64,6,2048]{2,1,0:T(8,128)(2,1)}), bf16[64,6,2048]{2,1,0:T(8,128)(2,1)S(1)}, u32[]{:S(2)}, u32[]{:S(2)}) async-start(bf16[64,6,2048]{2,1,0:T(8,128)(2,1)} %all_to_all.32), calls=%async_computation | async-start | bytes 4194304 | tf_op jit(solution)/shard_map/all_to_all | solution.py:53
  81.2 0.8 copy-start.3
  104.2 1.3 copy-start.2
  105.5 57.2 %all-to-all-start.2 = ((bf16[64,6,2048]{2,1,0:T(8,128)(2,1)}), bf16[64,6,2048]{2,1,0:T(8,128)(2,1)}, u32[]{:S(2)}, u32[]{:S(2)}) async-start(bf16[64,6,2048]{2,1,0:T(8,128)(2,1)} %all_to_all.38), calls=%async_computation.3 | async-start | bytes 4194304 | tf_op jit(solution)/shard_map/all_to_all | solution.py:54
  116.4 1.9 copy-start.12
  118.3 2.0 copy-start.8
  119.0 0.7 copy-start.9
  162.7 57.1 %all-to-all-start.1 = ((bf16[64,6,2048]{2,1,0:T(8,128)(2,1)}), bf16[64,6,2048]{2,1,0:T(8,128)(2,1)S(1)}, u32[]{:S(2)}, u32[]{:S(2)}) async-start(bf16[64,6,2048]{2,1,0:T(8,128)(2,1)} %all_to_all.35), calls=%async_computation.1 | async-start | bytes 4194304 | tf_op jit(solution)/shard_map/all_to_all | solution.py:104
  174.5 2.3 copy-start.11
  174.5 2.3 copy-start.13
  219.7 1.3 copy-start.1
  221.0 57.1 %all-to-all-start.3 = ((bf16[64,6,2048]{2,1,0:T(8,128)(2,1)}), bf16[64,6,2048]{2,1,0:T(8,128)(2,1)S(1)}, u32[]{:S(2)}, u32[]{:S(2)}) async-start(bf16[64,6,2048]{2,1,0:T(8,128)(2,1)} %all_to_all.41), calls=%async_computation.4 | async-start | bytes 4194304 | tf_op jit(solution)/shard_map/all_to_all | solution.py:105
  229.2 53.6 %reduce-scatter.3.cloned.1.call-start = ((), (), s32[]{:S(2)}) async-start(), calls=%async_computation.6 | async-start | bytes 1179648 | tf_op jit(solution)/shard_map/reduce_scatter | solution.py:122
  229.4 3.1 copy-start.5
  230.9 1.5 copy-start.10
  237.6 3.9 %copy-start.4 = (bf16[128,2048]{1,0:T(8,128)(2,1)S(1)}, bf16[128,2048]{1,0:T(8,128)(2,1)}, u32[]{:S(2)}) copy-start(bf16[128,2048]{1,0:T(8,128)(2,1)} %copy-done.3) | copy-start | bytes 1572868
  241.5 83.5 %reduce-scatter.5.cloned.1.call-start = ((), (), s32[]{:S(2)}) async-start(), calls=%async_computation.7 | async-start | bytes 1179648 | tf_op jit(solution)/shard_map/reduce_scatter | solution.py:123
  241.5 1.6 copy-start.6
  241.5 2.8 copy-start.7
Sparse Core Ops, SparseCore 0:
  241.6 40.3 reduce-scatter.2
  284.7 40.1 reduce-scatter.4
where the time goes:
time: 335 us; the launch traced here: 333 us
  waiting for transfers between devices  168 us (50%)
  blocking collectives  52.7 us (16%)
  starting transfers between devices  38.9 us (12%)
  local copies, waits for them, and re-layouts  28.1 us (8%)
  matrix products  25.5 us (8%)
  between operations  14.4 us (4%)
  other arithmetic  6.19 us (2%)
    all_to_all x1, waiting for transfers between devices, on_device(): lax.all_to_all(g_slots, 'expert', split_axis=0, concat_axis=0, tiled=True)  40.8 us
    reduce_scatter x1, waiting for transfers between devices, on_device(): lax.psum_scatter(early_input, 'tensor', scatter_dimension=1, tiled=True)  40.7 us
    all_to_all x1, waiting for transfers between devices, on_device(): lax.all_to_all(value_part, 'expert', split_axis=0, concat_axis=0, tiled=T...  37 us
    all_to_all x1, waiting for transfers between devices, on_device(): lax.all_to_all(input_part, 'expert', split_axis=0, concat_axis=0, tiled=T...  32.4 us
    all_gather x1, blocking collectives, on_device(): lax.all_gather(tokens, 'tensor', axis=1, tiled=True)  27.1 us
    all_gather x1, blocking collectives, on_device(): lax.all_gather(cotangent, 'tensor', axis=1, tiled=True)  25.5 us
    all_to_all x1, waiting for transfers between devices, on_device(): lax.all_to_all(x_slots, 'expert', split_axis=0, concat_axis=0, tiled=True)  16.7 us
    all_to_all x1, starting transfers between devices, on_device(): lax.all_to_all(x_slots, 'expert', split_axis=0, concat_axis=0, tiled=True)  14.1 us
  transfers between devices with their start and end apart: 6, of which 5 were waited for; matrix products, arithmetic and copies ran while one was open for 8% of the time, Pallas kernels for 0%

commit v1 on v0

v1 whole, which is shorter than its diff:
```python
import functools

import jax
import jax.numpy as jnp
from jax import lax
from jax.experimental import pallas as pl
from jax.experimental.pallas import tpu as pltpu
from jax.sharding import PartitionSpec as P

MESH = pl.DeviceIdType.MESH
F32 = jnp.float32
BF16 = jnp.bfloat16
CAP = 6
Z_SIZE = 8
OWN_ROWS = tuple(range(6))
SIB_ROWS = tuple(range(6))
NB = 16


def nt_dot(a, b):
    return lax.dot_general(a, b, (((1,), (1,)), ((), ())), preferred_element_type=F32)


def nn_dot(a, b):
    return jnp.dot(a, b, preferred_element_type=F32)


def silu_parts(v):
    s = jax.nn.sigmoid(v)
    return v * s, s * (1.0 + v * (1.0 - s))


def slot_ranks(shape, first, ranks):
    i = lax.broadcasted_iota(jnp.int32, shape, 1)
    inside = (i >= first) & (i < first + len(ranks))
    return jnp.where(inside, i - first + ranks[0], -1).astype(F32)


def kernel(
    dims,
    tok,
    cot,
    ids,
    wts,
    sg_h,
    su_h,
    sd_h,
    eg_h,
    eu_h,
    ed_h,
    out_v,
    out_i,
    sg,
    su,
    sd,
    eg,
    eu,
    ed,
    meta_out,
    meta_in,
    sib,
    full,
    b_send,
    b_recv,
    b_full,
    r_out,
    r_in,
    t_out,
    t_in,
    ret_send,
    ret_recv,
    fin_out,
    fin_in,
    acc_s,
    acc_b,
    comb,
    w_sem,
    sib_send,
    sib_recv,
    ag_send,
    ag_recv,
    rs_send,
    rs_recv,
    a2a_send,
    a2a_recv,
):
    nq, nx, nz, ny = dims
    t_rows, lanes = tok.shape
    hid = sg.shape[0]
    half = ny // 2
    e_me = lax.axis_index("expert")
    y = lax.axis_index("tensor")
    core = e_me % 2
    q = e_me // 2
    x = q // nz
    z = q % nz
    sibling = (e_me + 1 - 2 * core, y)
    sides = ((e_me, (y + 1) % ny), (e_me, (y + ny - 1) % ny))

    def at_offset(d, sign):
        dx = d // nz
        dz = d % nz
        xx = (x + sign * dx + nx) % nx
        zz = (z + sign * dz + nz) % nz
        return (2 * (xx * nz + zz) + core, y)

    loads = [
        pltpu.make_async_copy(h, v, w_sem.at[k])
        for k, (h, v) in enumerate(
            ((sg_h, sg), (su_h, su), (sd_h, sd), (eg_h, eg), (eu_h, eu), (ed_h, ed))
        )
    ]
    for load in loads:
        load.start()

    barrier = pltpu.get_barrier_semaphore()

    @pl.loop(1, nq)
    def _(d):
        pl.semaphore_signal(barrier, inc=1, device_id=at_offset(d, 1), device_id_type=MESH)

    for dev in (sibling, *sides):
        pl.semaphore_signal(barrier, inc=1, device_id=dev, device_id_type=MESH)

    full[0, y] = tok[...]
    full[1, y] = cot[...]

    lane = lax.broadcasted_iota(jnp.int32, (t_rows, 128), 1)
    d_of = lane % nq
    xx = (x + d_of // nz) % nx
    zz = (z + d_of % nz) % nz
    to_core = jnp.where(lane < nq, core, 1 - core)
    e_of = jnp.where(lane < 2 * nq, 2 * (xx * nz + zz) + to_core, -1)
    named = jnp.zeros((t_rows, 128), F32)
    weight = jnp.zeros((t_rows, 128), F32)
    for k in range(ids.shape[1]):
        hit = ids[:, k : k + 1] == e_of
        named = named + jnp.where(hit, 1.0, 0.0)
        weight = weight + jnp.where(hit, wts[:, k : k + 1], 0.0)
    row = lax.broadcasted_iota(jnp.int32, (t_rows, t_rows), 0)
    col = lax.broadcasted_iota(jnp.int32, (t_rows, t_rows), 1)
    before = jnp.where(col < row, 1.0, 0.0).astype(BF16)
    rank = nn_dot(before, named.astype(BF16))
    rank_t = jnp.where(named > 0.0, rank, 1000.0).T
    weight_t = weight.T
    meta_out[0] = rank_t[nq : 2 * nq]
    meta_out[1] = weight_t[nq : 2 * nq]

    pl.semaphore_wait(barrier, nq + 2)

    def send(src, dst, s_sem, r_sem, dev):
        return pltpu.make_async_remote_copy(
            src_ref=src, dst_ref=dst, send_sem=s_sem, recv_sem=r_sem, device_id=dev, device_id_type=MESH
        )

    to_sib = [
        send(meta_out, meta_in, sib_send.at[0], sib_recv.at[0], sibling),
        send(tok, sib.at[0], sib_send.at[1], sib_recv.at[1], sibling),
        send(cot, sib.at[1], sib_send.at[2], sib_recv.at[2], sibling),
    ]
    for copy in to_sib:
        copy.start()

    def steps_of(kind, way):
        return half if (kind + way) % 2 == 0 else half - 1

    def ag_copy(buf, group, kind, way, s):
        blk = (y + (ny - s if way == 0 else s)) % ny
        at = buf.at[kind, blk]
        return send(at, at, ag_send.at[group, kind, way, s], ag_recv.at[group, kind, way, s], sides[way])

    def ag_block(way, s):
        return (y + (ny - 1 - s if way == 0 else 1 + s)) % ny

    pairs = [(kind, way) for kind in range(2) for way in range(2)]

    def cols(ref, blk):
        return ref[:, pl.ds(pl.multiple_of(blk * lanes, lanes), lanes)]

    def shared_first(kind, blk, first=False):
        v = full[kind, blk]
        for k, w in ((0, sg), (1, su)) if kind == 0 else ((2, sd),):
            term = nt_dot(v, cols(w, blk))
            acc_s[k] = term if first else acc_s[k] + term

    def routed_first(kind, blk, first=False):
        v = b_full[kind, blk]
        for k, w in ((0, eg), (1, eu)) if kind == 0 else ((2, ed),):
            term = nt_dot(v, cols(w, blk))
            acc_b[k] = term if first else acc_b[k] + term

    def gather(buf, group, compute, begun=False):
        for s in range(half):
            for kind, way in pairs:
                if s < steps_of(kind, way) and not (begun and s == 0):
                    if s > 0:
                        ag_copy(buf, group, kind, way, s - 1).wait_recv()
                    ag_copy(buf, group, kind, way, s).start()
            for kind, way in pairs:
                if s == 0:
                    if way == 0:
                        compute(kind, y, True)
                elif s < steps_of(kind, way):
                    compute(kind, ag_block(way, s - 1))
        for kind, way in pairs:
            n = steps_of(kind, way)
            if n < half:
                ag_copy(buf, group, kind, way, n - 1).wait_recv()
                compute(kind, ag_block(way, n - 1))
        for kind, way in pairs:
            n = steps_of(kind, way)
            if n == half:
                ag_copy(buf, group, kind, way, n - 1).wait_recv()
                compute(kind, ag_block(way, n - 1))
        for kind, way in pairs:
            for s in range(steps_of(kind, way)):
                ag_copy(buf, group, kind, way, s).wait_send()

    for kind, way in pairs:
        ag_copy(full, 0, kind, way, 0).start()

    shape = (nq, NB, t_rows)
    own_rank = slot_ranks(shape, 0, OWN_ROWS)
    sib_rank = slot_ranks(shape, len(OWN_ROWS), SIB_ROWS)

    def place(rank_rows, weight_rows, wanted):
        pick = jnp.where(rank_rows.reshape(nq, 1, t_rows) == wanted, 1.0, 0.0)
        scaled = pick * weight_rows.reshape(nq, 1, t_rows)
        return pick.reshape(nq * NB, t_rows), scaled.reshape(nq * NB, t_rows)

    own_pick, own_scaled = place(rank_t[:nq], weight_t[:nq], own_rank)
    for copy in to_sib:
        copy.wait_recv()
    sib_pick, sib_scaled = place(meta_in[0], meta_in[1], sib_rank)
    slot_weight = jnp.sum(own_scaled, axis=1, keepdims=True) + jnp.sum(sib_scaled, axis=1, keepdims=True)
    own_bf, sib_bf = own_pick.astype(BF16), sib_pick.astype(BF16)
    x_rows = nn_dot(own_bf, tok[...]) + nn_dot(sib_bf, sib[0])
    g_rows = slot_weight * (nn_dot(own_bf, cot[...]) + nn_dot(sib_bf, sib[1]))
    slabs = jnp.concatenate((x_rows.reshape(nq, NB, lanes), g_rows.reshape(nq, NB, lanes)), axis=1)
    b_send[...] = slabs.astype(BF16)

    def out_copy(d):
        return send(b_send.at[d], b_recv.at[d], a2a_send.at[0, d], a2a_recv.at[0, d], at_offset(d, 1))

    @pl.loop(1, nq)
    def _(d):
        out_copy(d).start()

    b_recv[0] = b_send[0]

    for k, (pick, scaled) in enumerate(((own_pick, own_scaled), (sib_pick, sib_scaled))):
        high = scaled.astype(BF16).astype(F32)
        comb[k, 0] = pick.T.astype(BF16)
        comb[k, 1] = high.T.astype(BF16)
        comb[k, 2] = (scaled - high).T.astype(BF16)

    for load in loads[:3]:
        load.wait()
    gather(full, 0, shared_first, begun=True)

    @pl.loop(1, nq)
    def _(d):
        out_copy(d).wait_recv()

    arrived = b_recv[...].astype(F32)
    b_full[0, y] = arrived[:, :NB].reshape(nq * NB, lanes).astype(BF16)
    b_full[1, y] = arrived[:, NB:].reshape(nq * NB, lanes).astype(BF16)
    for load in loads[3:]:
        load.wait()
    gather(b_full, 1, routed_first)

    def middle(acc):
        gate, up, grad = acc[0], acc[1], acc[2]
        act, slope = silu_parts(gate)
        return (
            (act * up).astype(BF16),
            (grad * up * slope).astype(BF16),
            (grad * act).astype(BF16),
        )

    hidden_b, gate_b, up_b = middle(acc_b)

    def routed_second(kind, blk):
        if kind == 0:
            return nn_dot(hidden_b, cols(ed, blk))
        return nn_dot(gate_b, cols(eg, blk)) + nn_dot(up_b, cols(eu, blk))

    def rs_target(kind, way, s):
        far = steps_of(kind, way) - s
        return (y + (far if way == 0 else ny - far)) % ny

    def rs_copy(o, i, group, kind, way, s):
        return send(
            o.at[kind, way, s],
            i.at[kind, way, s],
            rs_send.at[group, kind, way, s],
            rs_recv.at[group, kind, way, s],
            sides[way],
        )

    def scatter(o, i, group, compute):
        for s in range(half):
            for kind, way in pairs:
                if s < steps_of(kind, way):
                    term = compute(kind, rs_target(kind, way, s))
                    if s > 0:
                        rs_copy(o, i, group, kind, way, s - 1).wait_recv()
                        term = term + i[kind, way, s - 1].astype(F32)
                    o[kind, way, s] = term.astype(BF16)
                    rs_copy(o, i, group, kind, way, s).start()
        totals = []
        for kind in range(2):
            total = compute(kind, y)
            for way in range(2):
                n = steps_of(kind, way)
                rs_copy(o, i, group, kind, way, n - 1).wait_recv()
                total = total + i[kind, way, n - 1].astype(F32)
            totals.append(total)
        return totals

    def scatter_end(o, i, group):
        for kind, way in pairs:
            for s in range(steps_of(kind, way)):
                rs_copy(o, i, group, kind, way, s).wait_send()

    value_b, input_b = scatter(r_out, r_in, 0, routed_second)
    slabs = jnp.concatenate((value_b.reshape(nq, NB, lanes), input_b.reshape(nq, NB, lanes)), axis=1)
    ret_send[...] = slabs.astype(BF16)

    def back_copy(d):
        return send(ret_send.at[d], ret_recv.at[d], a2a_send.at[1, d], a2a_recv.at[1, d], at_offset(d, -1))

    @pl.loop(1, nq)
    def _(d):
        back_copy(d).start()

    ret_recv[0] = ret_send[0]

    hidden_s, gate_s, up_s = middle(acc_s)

    def shared_second(kind, blk):
        if kind == 0:
            return nn_dot(hidden_s, cols(sd, blk))
        return nn_dot(gate_s, cols(sg, blk)) + nn_dot(up_s, cols(su, blk))

    value_t, input_t = scatter(t_out, t_in, 1, shared_second)

    @pl.loop(1, nq)
    def _(d):
        back_copy(d).wait_recv()

    arrived = ret_recv[...].astype(F32)
    value_r = arrived[:, :NB].reshape(nq * NB, lanes).astype(BF16)
    input_r = arrived[:, NB:].reshape(nq * NB, lanes).astype(BF16)

    fin_out[0] = nn_dot(comb[1, 1], value_r) + nn_dot(comb[1, 2], value_r)
    fin_out[1] = nn_dot(comb[1, 0], input_r)
    last = send(fin_out, fin_in, sib_send.at[3], sib_recv.at[3], sibling)
    last.start()
    value_t = value_t + nn_dot(comb[0, 1], value_r) + nn_dot(comb[0, 2], value_r)
    input_t = input_t + nn_dot(comb[0, 0], input_r)
    last.wait_recv()
    out_v[...] = (value_t + fin_in[0]).astype(BF16)
    out_i[...] = (input_t + fin_in[1]).astype(BF16)

    scatter_end(r_out, r_in, 0)
    scatter_end(t_out, t_in, 1)
    for copy in (*to_sib, last):
        copy.wait_send()

    @pl.loop(1, nq)
    def _(d):
        out_copy(d).wait_send()
        back_copy(d).wait_send()


def on_device(*args):
    tokens, cotangent, route_ids, route_weights, sg, su, sd, eg, eu, ed = args
    ny = lax.axis_size("tensor")
    nq = lax.axis_size("expert") // 2
    nz = min(Z_SIZE, nq)
    t_rows, lanes = tokens.shape
    hid, feats = sg.shape
    half = ny // 2
    eg, eu, ed = (w.reshape(hid, feats) for w in (eg, eu, ed))
    rows = nq * NB
    vmem, dma = pltpu.VMEM, pltpu.SemaphoreType.DMA
    out = jax.ShapeDtypeStruct((t_rows, lanes), BF16)
    in_vmem = pl.BlockSpec(memory_space=pltpu.VMEM)
    in_any = pl.BlockSpec(memory_space=pl.ANY)
    return pl.pallas_call(
        functools.partial(kernel, (nq, nq // nz, nz, ny)),
        out_shape=(out, out),
        in_specs=[in_vmem] * 4 + [in_any] * 6,
        out_specs=(in_vmem, in_vmem),
        scratch_shapes=[
            *[vmem((hid, feats), BF16)] * 6,
            vmem((2, nq, t_rows), F32),
            vmem((2, nq, t_rows), F32),
            vmem((2, t_rows, lanes), BF16),
            vmem((2, ny, t_rows, lanes), BF16),
            vmem((nq, 2 * NB, lanes), BF16),
            vmem((nq, 2 * NB, lanes), BF16),
            vmem((2, ny, rows, lanes), BF16),
            vmem((2, 2, half, rows, lanes), BF16),
            vmem((2, 2, half, rows, lanes), BF16),
            vmem((2, 2, half, t_rows, lanes), BF16),
            vmem((2, 2, half, t_rows, lanes), BF16),
            vmem((nq, 2 * NB, lanes), BF16),
            vmem((nq, 2 * NB, lanes), BF16),
            vmem((2, t_rows, lanes), F32),
            vmem((2, t_rows, lanes), F32),
            vmem((3, t_rows, hid), F32),
            vmem((3, rows, hid), F32),
            vmem((2, 3, t_rows, rows), BF16),
            dma((6,)),
            dma((4,)),
            dma((4,)),
            dma((2, 2, 2, half)),
            dma((2, 2, 2, half)),
            dma((2, 2, 2, half)),
            dma((2, 2, 2, half)),
            dma((2, nq)),
            dma((2, nq)),
        ],
        compiler_params=pltpu.CompilerParams(
            collective_id=0, has_side_effects=True, vmem_limit_bytes=56 * 2**20
        ),
        name="routed_layer",
    )(tokens, cotangent, route_ids, route_weights, sg, su, sd, eg, eu, ed)


def solution(mesh):
    in_specs = (
        P("expert", "tensor"),
        P("expert", "tensor"),
        P("expert", None),
        P("expert", None),
        P("tensor", None),
        P("tensor", None),
        P("tensor", None),
        P("expert", "tensor", None),
        P("expert", "tensor", None),
        P("expert", "tensor", None),
    )
    out_specs = (P("expert", "tensor"), P("expert", "tensor"))
    return jax.shard_map(
        on_device, mesh=mesh, in_specs=in_specs, out_specs=out_specs, check_vma=False
    )
```

time: 335 us -> 148 us (0.44)
  waiting for transfers between devices: 168 us -> 0 us
  Pallas kernels: 0 us -> 141 us
  blocking collectives: 52.7 us -> 0 us
  starting transfers between devices: 38.9 us -> 0 us
  matrix products: 25.5 us -> 0 us
  local copies, waits for them, and re-layouts: 28.1 us -> 4.3 us
  between operations: 14.4 us -> 0.66 us
  other arithmetic: 6.19 us -> 0 us
    pallas_call x0 -> x1, Pallas kernels: none -> 141 us  [on_device(): pl.pallas_call(functools.partial(kernel, (nq, nq // nz, nz, ny)), out_sha...]
    all_to_all x4 -> x0, waiting for transfers between devices: 127 us -> none  [the longest x1 40.8 us: on_device(): lax.all_to_all(g_slots, 'expert', split_axis=0, concat_axis=0, tiled=True)]
    all_gather x2 -> x0, blocking collectives: 52.7 us -> none  [the longest x1 27.1 us: on_device(): lax.all_gather(tokens, 'tensor', axis=1, tiled=True)]
    reduce_scatter x2 -> x0, waiting for transfers between devices: 40.7 us -> none  [the longest x1 40.7 us: on_device(): lax.psum_scatter(early_input, 'tensor', scatter_dimension=1, tiled=True)]
    all_to_all x4 -> x0, starting transfers between devices: 38.7 us -> none  [the longest x1 14.1 us: on_device(): lax.all_to_all(x_slots, 'expert', split_axis=0, concat_axis=0, tiled=True)]
    dot_general x15 -> x0, matrix products: 25.5 us -> none  [the longest x1 3.87 us: on_device(): jnp.einsum('st,sd->td', gate_dispatch, value_back.astype(jnp.float32), pr...]
    all_to_all x8 -> x0, local copies, waits for them, and re-layouts: 22 us -> none  [the longest x2 7.41 us: on_device(): lax.all_to_all(g_slots, 'expert', split_axis=0, concat_axis=0, tiled=True)]
  transfers between devices with their start and end apart: 6 -> 0, of which waited for: 5 -> 0; matrix products, arithmetic and copies ran while one was open for 8% -> 0% of each run, Pallas kernels for 0% -> 0%
where the time goes in v1:
time: 148 us; the launch traced here: 146 us
  Pallas kernels  141 us (95%)
  local copies, waits for them, and re-layouts  4.3 us (3%)
    pallas_call x1, Pallas kernels, on_device(): pl.pallas_call(functools.partial(kernel, (nq, nq // nz, nz, ny)), out_sha...  141 us
    unnamed x10, local copies, waits for them, and re-layouts  4.3 us

profile of v1, /device:TPU:6, one launch (start us, length us, event | category | flops | bytes accessed | tf_op | source)
XLA Modules:
  0.0 145.6 jit_solution(3653513097122530319)
XLA Ops:
  0.6 0.0 copy-start.1
  0.6 0.7 copy-done.1
  1.3 0.0 copy-start.2
  1.3 0.7 copy.12.ids
  2.1 0.0 copy-done.2
  2.1 0.7 copy.13.wts
  2.8 140.6 %routed_layer.1 = (bf16[128,256]{1,0:T(8,128)(2,1)}, bf16[128,256]{1,0:T(8,128)(2,1)}) custom-call(bf16[128,256]{1,0:T(8,128)(2,1)} %tok.1, bf16[128,256]{1,0:T(8,128)(2,1)} %cot.1, s32[128,6]{1,0:T(8,128)} %copy.12.ids, f32[128,6]{1,0:T(8,128)} %copy.13.wts, bf16[176,2048]{1,0:T(8,128)(2,1)} %sg_h.1, bf16[176,2048]{1,0:T(8,128)(2,1)} %su_h.1, ...), custom_call_target="tpu_custom_call" | custom-call | tf_op jit(solution)/shard_map/routed_layer/pallas_call | solution.py:391
  143.4 0.0 copy-start
  143.4 1.5 %copy.16 = bf16[128,256]{1,0:T(8,128)(2,1)} copy(bf16[128,256]{1,0:T(8,128)(2,1)} %get-tuple-element.4) | data formatting | bytes 131072
  144.9 0.0 copy-done
  144.9 0.6 copy.17
Async XLA Ops:
  0.6 0.7 copy-start.1
  1.3 0.7 copy-start.2
  143.4 1.5 %copy-start = (bf16[128,256]{1,0:T(8,128)(2,1)S(1)}, bf16[128,256]{1,0:T(8,128)(2,1)}, u32[]{:S(2)}) copy-start(bf16[128,256]{1,0:T(8,128)(2,1)} %get-tuple-element.5) | copy-start | bytes 196612

commit v2 on v1

v2 whole, which is shorter than its diff:
```python
import functools

import jax
import jax.numpy as jnp
from jax import lax
from jax.experimental import pallas as pl
from jax.experimental.pallas import tpu as pltpu
from jax.sharding import PartitionSpec as P

MESH = pl.DeviceIdType.MESH
F32 = jnp.float32
BF16 = jnp.bfloat16
CAP = 6
Z_SIZE = 8
WIDE = 4
OWN_ROWS = (4, 5)
SIB_ROWS = (0, 1, 2, 3, 4, 5)
NB = len(OWN_ROWS) + len(SIB_ROWS)
NA = 2 * WIDE
NEAR = 3


def nt_dot(a, b):
    return lax.dot_general(a, b, (((1,), (1,)), ((), ())), preferred_element_type=F32)


def nn_dot(a, b):
    return jnp.dot(a, b, preferred_element_type=F32)


def silu_parts(v):
    s = jax.nn.sigmoid(v)
    return v * s, s * (1.0 + v * (1.0 - s))


def slot_ranks(shape, first, ranks):
    i = lax.broadcasted_iota(jnp.int32, shape, 1)
    inside = (i >= first) & (i < first + len(ranks))
    return jnp.where(inside, i - first + ranks[0], -1).astype(F32)


def kernel(
    dims,
    tok,
    cot,
    ids,
    wts,
    sg_h,
    su_h,
    sd_h,
    eg_h,
    eu_h,
    ed_h,
    out_v,
    out_i,
    sg,
    su,
    sd,
    eg,
    eu,
    ed,
    meta_out,
    meta_in,
    sib,
    full,
    b_send,
    b_recv,
    b_full,
    r_out,
    r_in,
    t_out,
    t_in,
    ret_send,
    ret_recv,
    near_send,
    far_send,
    near_recv,
    far_recv,
    near_back,
    far_back,
    near_home,
    far_home,
    fin_out,
    fin_in,
    acc_s,
    acc_b,
    acc_a,
    comb,
    comb_a,
    w_sem,
    sib_send,
    sib_recv,
    ag_send,
    ag_recv,
    rs_send,
    rs_recv,
    a2a_send,
    a2a_recv,
):
    nq, nx, nz, ny = dims
    t_rows, lanes = tok.shape
    half = ny // 2
    e_me = lax.axis_index("expert")
    y = lax.axis_index("tensor")
    core = e_me % 2
    q = e_me // 2
    x = q // nz
    z = q % nz
    sibling = (e_me + 1 - 2 * core, y)
    sides = ((e_me, (y + 1) % ny), (e_me, (y + ny - 1) % ny))
    pairs = [(kind, way) for kind in range(2) for way in range(2)]
    offsets = [0]
    for s in range(1, half):
        offsets += [-s, s]
    offsets += [half]

    def block_at(off):
        return (y + off + ny) % ny

    def at_offset(d, sign):
        dx = d // nz
        dz = d % nz
        xx = (x + sign * dx + nx) % nx
        zz = (z + sign * dz + nz) % nz
        return (2 * (xx * nz + zz) + core, y)

    def send(src, dst, s_sem, r_sem, dev):
        return pltpu.make_async_remote_copy(
            src_ref=src, dst_ref=dst, send_sem=s_sem, recv_sem=r_sem, device_id=dev, device_id_type=MESH
        )

    def cols(ref, blk):
        return ref[:, pl.ds(pl.multiple_of(blk * lanes, lanes), lanes)]

    loads = [
        pltpu.make_async_copy(h, v, w_sem.at[k])
        for k, (h, v) in enumerate(
            ((sg_h, sg), (su_h, su), (sd_h, sd), (eg_h, eg), (eu_h, eu), (ed_h, ed))
        )
    ]
    for load in loads:
        load.start()

    barrier = pltpu.get_barrier_semaphore()

    @pl.loop(1, nq)
    def _(d):
        pl.semaphore_signal(barrier, inc=1, device_id=at_offset(d, 1), device_id_type=MESH)

    for dev in (sibling, *sides):
        pl.semaphore_signal(barrier, inc=1, device_id=dev, device_id_type=MESH)

    full[0, y] = tok[...]
    full[1, y] = cot[...]

    line = lax.broadcasted_iota(jnp.int32, (2 * nq, t_rows), 0)
    d_of = line % nq
    xx = (x + d_of // nz) % nx
    zz = (z + d_of % nz) % nz
    e_of = 2 * (xx * nz + zz) + jnp.where(line < nq, core, 1 - core)
    named = jnp.zeros((2 * nq, t_rows), F32)
    weight = jnp.zeros((2 * nq, t_rows), F32)
    for k in range(ids.shape[0]):
        hit = ids[k : k + 1, :] == e_of
        named = named + jnp.where(hit, 1.0, 0.0)
        weight = weight + jnp.where(hit, wts[k : k + 1, :], 0.0)
    row = lax.broadcasted_iota(jnp.int32, (t_rows, t_rows), 0)
    col = lax.broadcasted_iota(jnp.int32, (t_rows, t_rows), 1)
    before = jnp.where(row < col, 1.0, 0.0).astype(BF16)
    rank = jnp.where(named > 0.0, nn_dot(named.astype(BF16), before), 1000.0)
    meta_out[0] = rank[nq:]
    meta_out[1] = weight[nq:]

    pl.semaphore_wait(barrier, nq + 2)

    to_sib = [
        send(meta_out, meta_in, sib_send.at[0], sib_recv.at[0], sibling),
        send(tok, sib.at[0], sib_send.at[1], sib_recv.at[1], sibling),
        send(cot, sib.at[1], sib_send.at[2], sib_recv.at[2], sibling),
    ]
    for copy in to_sib:
        copy.start()

    def steps_of(kind, way):
        return half if (kind + way) % 2 == 0 else half - 1

    def ag_copy(buf, group, kind, way, s):
        at = buf.at[kind, block_at(-s if way == 0 else s)]
        return send(at, at, ag_send.at[group, kind, way, s], ag_recv.at[group, kind, way, s], sides[way])

    def ag_start(buf, group):
        for kind, way in pairs:
            ag_copy(buf, group, kind, way, 0).start()

    def ag_step(buf, group, s):
        for kind, way in pairs:
            ag_copy(buf, group, kind, way, s - 1).wait_recv()
            if s < steps_of(kind, way):
                ag_copy(buf, group, kind, way, s).start()

    def ag_last(buf, group):
        for kind, way in pairs:
            if steps_of(kind, way) == half:
                ag_copy(buf, group, kind, way, half - 1).wait_recv()

    def ag_end(buf, group):
        for kind, way in pairs:
            for s in range(steps_of(kind, way)):
                ag_copy(buf, group, kind, way, s).wait_send()

    ag_start(full, 0)

    def first_layer(acc, v, g, weights, blk, first):
        gate, up, down = weights
        for k, (rows, w) in enumerate(((v, gate), (v, up), (g, down))):
            term = nt_dot(rows, cols(w, blk))
            acc[k] = term if first else acc[k] + term

    def shared_first(off):
        blk = block_at(off)
        first_layer(acc_s, full[0, blk], full[1, blk], (sg, su, sd), blk, off == 0)

    def routed_first(off):
        blk = block_at(off)
        first_layer(acc_b, b_full[0, blk], b_full[1, blk], (eg, eu, ed), blk, off == 0)

    shape = (nq, NB, t_rows)
    own_rank = slot_ranks(shape, 0, OWN_ROWS)
    sib_rank = slot_ranks(shape, len(OWN_ROWS), SIB_ROWS)

    def place(rank_rows, weight_rows, wanted):
        n = wanted.shape[1]
        pick = jnp.where(rank_rows.reshape(nq, 1, t_rows) == wanted, 1.0, 0.0)
        scaled = pick * weight_rows.reshape(nq, 1, t_rows)
        return pick.reshape(nq * n, t_rows), scaled.reshape(nq * n, t_rows)

    own_pick, own_scaled = place(rank[:nq], weight[:nq], own_rank)
    for copy in to_sib:
        copy.wait_recv()
    sib_pick, sib_scaled = place(meta_in[0], meta_in[1], sib_rank)
    slot_weight = jnp.sum(own_scaled, axis=1, keepdims=True) + jnp.sum(sib_scaled, axis=1, keepdims=True)
    own_bf, sib_bf = own_pick.astype(BF16), sib_pick.astype(BF16)
    x_rows = nn_dot(own_bf, tok[...]) + nn_dot(sib_bf, sib[0])
    g_rows = slot_weight * (nn_dot(own_bf, cot[...]) + nn_dot(sib_bf, sib[1]))
    slabs = jnp.concatenate((x_rows.reshape(nq, NB, lanes), g_rows.reshape(nq, NB, lanes)), axis=1)
    b_send[...] = slabs.astype(BF16)

    def swap_copy(k, src, dst, sign):
        def at(d):
            return send(src.at[d], dst.at[d], a2a_send.at[k, d], a2a_recv.at[k, d], at_offset(d, sign))

        return at

    def start_all(copy):
        @pl.loop(1, nq)
        def _(d):
            copy(d).start()

    def wait_all(copy):
        @pl.loop(1, nq)
        def _(d):
            copy(d).wait_recv()

    b_out = swap_copy(0, b_send, b_recv, 1)
    near_out = swap_copy(1, near_send, near_recv, 1)
    far_out = swap_copy(2, far_send, far_recv, 1)
    far_in = swap_copy(3, far_back, far_home, -1)
    near_in = swap_copy(4, near_back, near_home, -1)
    b_in = swap_copy(5, ret_send, ret_recv, -1)

    start_all(b_out)
    b_recv[0] = b_send[0]

    slot = lax.broadcasted_iota(jnp.int32, (nq, NA, t_rows), 1)
    wide_rank = jnp.where(slot < WIDE, slot, slot - WIDE).astype(F32)
    wide_pick, wide_scaled = place(rank[:nq], weight[:nq], wide_rank)
    slot = slot.reshape(nq * NA, t_rows)
    top = slot < WIDE
    x_pick = jnp.where(top, wide_pick, 0.0).astype(BF16)
    g_pick = jnp.where(top, 0.0, wide_pick).astype(BF16)
    slot = lax.broadcasted_iota(jnp.int32, (nq, NA, 1), 1).reshape(nq * NA, 1)
    row_scale = jnp.where(slot < WIDE, 1.0, jnp.sum(wide_scaled, axis=1, keepdims=True))

    def wide_rows(p):
        blk = block_at(offsets[p])
        rows = row_scale * (nn_dot(x_pick, full[0, blk]) + nn_dot(g_pick, full[1, blk]))
        rows = rows.reshape(nq, NA, lanes).astype(BF16)
        if p < NEAR:
            near_send[:, :, p * lanes : (p + 1) * lanes] = rows
        else:
            far_send[:, :, (p - NEAR) * lanes : (p - NEAR + 1) * lanes] = rows

    for load in loads[:3]:
        load.wait()
    wide_rows(0)
    shared_first(0)
    for s in range(1, half):
        ag_step(full, 0, s)
        for p in (2 * s - 1, 2 * s):
            wide_rows(p)
        if s == 1:
            start_all(near_out)
            near_recv[0] = near_send[0]
        for p in (2 * s - 1, 2 * s):
            shared_first(offsets[p])
    ag_last(full, 0)

    wait_all(b_out)
    arrived = b_recv[...].astype(F32)
    b_full[0, y] = arrived[:, :NB].reshape(nq * NB, lanes).astype(BF16)
    b_full[1, y] = arrived[:, NB:].reshape(nq * NB, lanes).astype(BF16)
    ag_start(b_full, 1)

    wide_rows(ny - 1)
    start_all(far_out)
    far_recv[0] = far_send[0]
    shared_first(half)

    for k, (pick, scaled) in enumerate(((own_pick, own_scaled), (sib_pick, sib_scaled))):
        high = scaled.astype(BF16).astype(F32)
        comb[k, 0] = pick.T.astype(BF16)
        comb[k, 1] = high.T.astype(BF16)
        comb[k, 2] = (scaled - high).T.astype(BF16)
    wide_scaled = jnp.where(top, wide_scaled, 0.0)
    high = wide_scaled.astype(BF16).astype(F32)
    comb_a[0] = jnp.where(top, 0.0, wide_pick).T.astype(BF16)
    comb_a[1] = high.T.astype(BF16)
    comb_a[2] = (wide_scaled - high).T.astype(BF16)

    def middle(gate, up, grad):
        act, slope = silu_parts(gate)
        return (
            (act * up).astype(BF16),
            (grad * up * slope).astype(BF16),
            (grad * act).astype(BF16),
        )

    def second_layer(mid, weights):
        hidden, grad_gate, grad_up = mid
        gate, up, down = weights

        def of(kind, blk):
            if kind == 0:
                return nn_dot(hidden, cols(down, blk))
            return nn_dot(grad_gate, cols(gate, blk)) + nn_dot(grad_up, cols(up, blk))

        return of

    for load in loads[3:]:
        load.wait()
    routed_first(0)
    for s in range(1, half):
        ag_step(b_full, 1, s)
        routed_first(-s)
        routed_first(s)
    shared_mid = middle(acc_s[0], acc_s[1], acc_s[2])
    ag_last(b_full, 1)
    routed_first(half)
    routed_second = second_layer(middle(acc_b[0], acc_b[1], acc_b[2]), (eg, eu, ed))

    def rs_offset(kind, way, s):
        far = steps_of(kind, way) - s
        return far if way == 0 else -far

    def rs_copy(o, i, group, kind, way, s):
        return send(
            o.at[kind, way, s],
            i.at[kind, way, s],
            rs_send.at[group, kind, way, s],
            rs_recv.at[group, kind, way, s],
            sides[way],
        )

    def rs_step(o, i, group, s, compute):
        for kind, way in pairs:
            if s < steps_of(kind, way):
                term = compute(kind, rs_offset(kind, way, s))
                if s > 0:
                    rs_copy(o, i, group, kind, way, s - 1).wait_recv()
                    term = term + i[kind, way, s - 1].astype(F32)
                o[kind, way, s] = term.astype(BF16)
                rs_copy(o, i, group, kind, way, s).start()

    def rs_total(o, i, group, compute):
        totals = []
        for kind in range(2):
            total = compute(kind, 0)
            for way in range(2):
                n = steps_of(kind, way)
                rs_copy(o, i, group, kind, way, n - 1).wait_recv()
                total = total + i[kind, way, n - 1].astype(F32)
            totals.append(total)
        return totals

    def rs_end(o, i, group):
        for kind, way in pairs:
            for s in range(steps_of(kind, way)):
                rs_copy(o, i, group, kind, way, s).wait_send()

    def routed_term(kind, off):
        return routed_second(kind, block_at(off))

    rs_step(r_out, r_in, 0, 0, routed_term)

    wait_all(near_out)
    for p in range(NEAR):
        blk = block_at(offsets[p])
        v = near_recv[:, :, p * lanes : (p + 1) * lanes].astype(F32).reshape(nq * NA, lanes).astype(BF16)
        first_layer(acc_a, v, v, (eg, eu, ed), blk, p == 0)
    wait_all(far_out)
    for p in range(NEAR, ny):
        blk = block_at(offsets[p])
        v = far_recv[:, :, (p - NEAR) * lanes : (p - NEAR + 1) * lanes]
        v = v.astype(F32).reshape(nq * NA, lanes).astype(BF16)
        first_layer(acc_a, v, v, (eg, eu, ed), blk, False)
    hid = sg.shape[0]
    slot = lax.broadcasted_iota(jnp.int32, (nq, NA, hid), 1).reshape(nq * NA, hid)
    top_hid = slot < WIDE
    gate_a, up_a = acc_a[0], acc_a[1]
    act, slope = silu_parts(gate_a)
    hidden_a = jnp.where(top_hid, act * up_a, 0.0).astype(BF16)

    def lowered(v):
        v = v.reshape(nq, NA, hid)
        return jnp.concatenate((v[:, WIDE:], v[:, :WIDE]), axis=1).reshape(nq * NA, hid)

    grad_a = acc_a[2]
    grad_gate_a = jnp.where(top_hid, 0.0, grad_a * lowered(up_a) * lowered(slope)).astype(BF16)
    grad_up_a = jnp.where(top_hid, 0.0, grad_a * lowered(act)).astype(BF16)
    wide_second = second_layer((hidden_a, grad_gate_a, grad_up_a), (eg, eu, ed))

    def wide_back(p):
        blk = block_at(offsets[p])
        rows = (wide_second(0, blk) + wide_second(1, blk)).reshape(nq, NA, lanes).astype(BF16)
        if p < NEAR:
            near_back[:, :, p * lanes : (p + 1) * lanes] = rows
        else:
            far_back[:, :, (p - NEAR) * lanes : (p - NEAR + 1) * lanes] = rows

    for p in range(NEAR, ny):
        wide_back(p)
    start_all(far_in)
    far_home[0] = far_back[0]
    for p in range(NEAR):
        wide_back(p)
    start_all(near_in)
    near_home[0] = near_back[0]

    for s in range(1, half):
        rs_step(r_out, r_in, 0, s, routed_term)
    value_b, input_b = rs_total(r_out, r_in, 0, routed_term)
    slabs = jnp.concatenate((value_b.reshape(nq, NB, lanes), input_b.reshape(nq, NB, lanes)), axis=1)
    ret_send[...] = slabs.astype(BF16)
    start_all(b_in)
    ret_recv[0] = ret_send[0]

    shared_second = second_layer(shared_mid, (sg, su, sd))

    def token_term(kind, off):
        p = offsets.index(off if -off != half else half)
        home, at = (near_home, p) if p < NEAR else (far_home, p - NEAR)
        rows = home[:, :, at * lanes : (at + 1) * lanes]
        rows = rows.astype(F32).reshape(nq * NA, lanes).astype(BF16)
        total = shared_second(kind, block_at(off))
        if kind == 0:
            return total + nn_dot(comb_a[1], rows) + nn_dot(comb_a[2], rows)
        return total + nn_dot(comb_a[0], rows)

    wait_all(far_in)
    near_from = half - 2
    for s in range(half):
        if s == near_from:
            wait_all(near_in)
        rs_step(t_out, t_in, 1, s, token_term)
    value_t, input_t = rs_total(t_out, t_in, 1, token_term)

    wait_all(b_in)
    arrived = ret_recv[...].astype(F32)
    value_r = arrived[:, :NB].reshape(nq * NB, lanes).astype(BF16)
    input_r = arrived[:, NB:].reshape(nq * NB, lanes).astype(BF16)

    fin_out[0] = nn_dot(comb[1, 1], value_r) + nn_dot(comb[1, 2], value_r)
    fin_out[1] = nn_dot(comb[1, 0], input_r)
    last = send(fin_out, fin_in, sib_send.at[3], sib_recv.at[3], sibling)
    last.start()
    value_t = value_t + nn_dot(comb[0, 1], value_r) + nn_dot(comb[0, 2], value_r)
    input_t = input_t + nn_dot(comb[0, 0], input_r)
    last.wait_recv()
    out_v[...] = (value_t + fin_in[0]).astype(BF16)
    out_i[...] = (input_t + fin_in[1]).astype(BF16)

    ag_end(full, 0)
    ag_end(b_full, 1)
    rs_end(r_out, r_in, 0)
    rs_end(t_out, t_in, 1)
    for copy in (*to_sib, last):
        copy.wait_send()

    @pl.loop(1, nq)
    def _(d):
        for copy in (b_out, near_out, far_out, far_in, near_in, b_in):
            copy(d).wait_send()


def on_device(*args):
    tokens, cotangent, route_ids, route_weights, sg, su, sd, eg, eu, ed = args
    ny = lax.axis_size("tensor")
    nq = lax.axis_size("expert") // 2
    nz = min(Z_SIZE, nq)
    t_rows, lanes = tokens.shape
    hid, feats = sg.shape
    half = ny // 2
    eg, eu, ed = (w.reshape(hid, feats) for w in (eg, eu, ed))
    rows = nq * NB
    vmem, dma = pltpu.VMEM, pltpu.SemaphoreType.DMA
    out = jax.ShapeDtypeStruct((t_rows, lanes), BF16)
    in_vmem = pl.BlockSpec(memory_space=pltpu.VMEM)
    in_any = pl.BlockSpec(memory_space=pl.ANY)
    return pl.pallas_call(
        functools.partial(kernel, (nq, nq // nz, nz, ny)),
        out_shape=(out, out),
        in_specs=[in_vmem] * 4 + [in_any] * 6,
        out_specs=(in_vmem, in_vmem),
        scratch_shapes=[
            *[vmem((hid, feats), BF16)] * 6,
            vmem((2, nq, t_rows), F32),
            vmem((2, nq, t_rows), F32),
            vmem((2, t_rows, lanes), BF16),
            vmem((2, ny, t_rows, lanes), BF16),
            vmem((nq, 2 * NB, lanes), BF16),
            vmem((nq, 2 * NB, lanes), BF16),
            vmem((2, ny, rows, lanes), BF16),
            vmem((2, 2, half, rows, lanes), BF16),
            vmem((2, 2, half, rows, lanes), BF16),
            vmem((2, 2, half, t_rows, lanes), BF16),
            vmem((2, 2, half, t_rows, lanes), BF16),
            vmem((nq, 2 * NB, lanes), BF16),
            vmem((nq, 2 * NB, lanes), BF16),
            *[vmem((nq, NA, n * lanes), BF16) for n in (NEAR, ny - NEAR)] * 4,
            vmem((2, t_rows, lanes), F32),
            vmem((2, t_rows, lanes), F32),
            vmem((3, t_rows, hid), F32),
            vmem((3, rows, hid), F32),
            vmem((3, nq * NA, hid), F32),
            vmem((2, 3, t_rows, rows), BF16),
            vmem((3, t_rows, nq * NA), BF16),
            dma((6,)),
            dma((4,)),
            dma((4,)),
            dma((2, 2, 2, half)),
            dma((2, 2, 2, half)),
            dma((2, 2, 2, half)),
            dma((2, 2, 2, half)),
            dma((6, nq)),
            dma((6, nq)),
        ],
        compiler_params=pltpu.CompilerParams(
            collective_id=0, has_side_effects=True, vmem_limit_bytes=56 * 2**20
        ),
        name="routed_layer",
    )(tokens, cotangent, route_ids.T, route_weights.T, sg, su, sd, eg, eu, ed)


def solution(mesh):
    in_specs = (
        P("expert", "tensor"),
        P("expert", "tensor"),
        P("expert", None),
        P("expert", None),
        P("tensor", None),
        P("tensor", None),
        P("tensor", None),
        P("expert", "tensor", None),
        P("expert", "tensor", None),
        P("expert", "tensor", None),
    )
    out_specs = (P("expert", "tensor"), P("expert", "tensor"))
    return jax.shard_map(
        on_device, mesh=mesh, in_specs=in_specs, out_specs=out_specs, check_vma=False
    )
```

time: 148 us -> 109 us (0.74)
  the two profiles are of different devices: /device:TPU:6 before, /device:TPU:1 now
where the time goes in v2:
time: 109 us
  Pallas kernels  106 us (97%)
  local copies, waits for them, and re-layouts  2.14 us (2%)
    pallas_call x1, Pallas kernels, on_device(): pl.pallas_call(functools.partial(kernel, (nq, nq // nz, nz, ny)), out_sha...  106 us

profile of v2, /device:TPU:1, one launch (start us, length us, event | category | flops | bytes accessed | tf_op | source)
XLA Modules:
  0.0 109.1 jit_solution(4767105031637124501)
XLA Ops:
  0.6 106.3 %routed_layer.1 = (bf16[128,256]{1,0:T(8,128)(2,1)}, bf16[128,256]{1,0:T(8,128)(2,1)}) custom-call(bf16[128,256]{1,0:T(8,128)(2,1)} %tok.1, bf16[128,256]{1,0:T(8,128)(2,1)} %cot.1, s32[6,128]{1,0:T(8,128)} %bitcast.8, f32[6,128]{1,0:T(8,128)} %bitcast.9, bf16[176,2048]{1,0:T(8,128)(2,1)} %sg_h.1, bf16[176,2048]{1,0:T(8,128)(2,1)} %su_h.1, ...), custom_call_target="tpu_custom_call" | custom-call | tf_op jit(solution)/shard_map/routed_layer/pallas_call | solution.py:519
  106.9 0.0 copy-start
  106.9 1.5 %copy.14 = bf16[128,256]{1,0:T(8,128)(2,1)} copy(bf16[128,256]{1,0:T(8,128)(2,1)} %get-tuple-element.4) | data formatting | bytes 131072
  108.4 0.0 copy-done
  108.4 0.6 copy.15
Async XLA Ops:
  106.9 1.5 %copy-start = (bf16[128,256]{1,0:T(8,128)(2,1)S(1)}, bf16[128,256]{1,0:T(8,128)(2,1)}, u32[]{:S(2)}) copy-start(bf16[128,256]{1,0:T(8,128)(2,1)} %get-tuple-element.5) | copy-start | bytes 196612

commit v3 on v2

--- a/solution.py
+++ b/solution.py
@@ -96,6 +96,7 @@
     rs_recv,
     a2a_send,
     a2a_recv,
+    round_sem,
 ):
     nq, nx, nz, ny = dims
     t_rows, lanes = tok.shape
@@ -115,13 +116,13 @@
     offsets += [half]
 
     def block_at(off):
-        return (y + off + ny) % ny
+        return lax.rem(y + off + ny, ny)
 
     def at_offset(d, sign):
-        dx = d // nz
-        dz = d % nz
-        xx = (x + sign * dx + nx) % nx
-        zz = (z + sign * dz + nz) % nz
+        dx = lax.div(d, nz) if not isinstance(d, int) else d // nz
+        dz = lax.rem(d, nz) if not isinstance(d, int) else d % nz
+        xx = lax.rem(x + dx if sign > 0 else x - dx + nx, nx)
+        zz = lax.rem(z + dz if sign > 0 else z - dz + nz, nz)
         return (2 * (xx * nz + zz) + core, y)
 
     def send(src, dst, s_sem, r_sem, dev):
@@ -131,6 +132,12 @@
 
     def cols(ref, blk):
         return ref[:, pl.ds(pl.multiple_of(blk * lanes, lanes), lanes)]
+
+    barrier = pltpu.get_barrier_semaphore()
+    column = [at_offset(k * nz, 1) for k in range(1, nx)]
+    greeted = [*sides, sibling, *column, *(at_offset(k, 1) for k in range(1, nz))]
+    for dev in greeted:
+        pl.semaphore_signal(barrier, inc=1, device_id=dev, device_id_type=MESH)
 
     loads = [
         pltpu.make_async_copy(h, v, w_sem.at[k])
@@ -141,17 +148,46 @@
     for load in loads:
         load.start()
 
-    barrier = pltpu.get_barrier_semaphore()
-
-    @pl.loop(1, nq)
-    def _(d):
-        pl.semaphore_signal(barrier, inc=1, device_id=at_offset(d, 1), device_id_type=MESH)
-
-    for dev in (sibling, *sides):
-        pl.semaphore_signal(barrier, inc=1, device_id=dev, device_id_type=MESH)
-
     full[0, y] = tok[...]
     full[1, y] = cot[...]
+
+    def steps_of(kind, way):
+        return half if (kind + way) % 2 == 0 else half - 1
+
+    def ag_copy(buf, group, kind, way, s):
+        at = buf.at[kind, block_at(-s if way == 0 else s)]
+        return send(at, at, ag_send.at[group, kind, way, s], ag_recv.at[group, kind, way, s], sides[way])
+
+    def ag_start(buf, group):
+        for kind, way in pairs:
+            ag_copy(buf, group, kind, way, 0).start()
+
+    def ag_step(buf, group, s):
+        for kind, way in pairs:
+            ag_copy(buf, group, kind, way, s - 1).wait_recv()
+            if s < steps_of(kind, way):
+                ag_copy(buf, group, kind, way, s).start()
+
+    def ag_last(buf, group):
+        for kind, way in pairs:
+            if steps_of(kind, way) == half:
+                ag_copy(buf, group, kind, way, half - 1).wait_recv()
+
+    def ag_end(buf, group):
+        for kind, way in pairs:
+            for s in range(steps_of(kind, way)):
+                ag_copy(buf, group, kind, way, s).wait_send()
+
+    pl.semaphore_wait(barrier, len(greeted))
+    ag_start(full, 0)
+    to_sib = [
+        send(tok, sib.at[0], sib_send.at[1], sib_recv.at[1], sibling),
+        send(cot, sib.at[1], sib_send.at[2], sib_recv.at[2], sibling),
+    ]
+    for copy in to_sib:
+        copy.start()
+    for dev in column:
+        pl.semaphore_signal(round_sem, inc=1, device_id=dev, device_id_type=MESH)
 
     line = lax.broadcasted_iota(jnp.int32, (2 * nq, t_rows), 0)
     d_of = line % nq
@@ -171,44 +207,8 @@
     meta_out[0] = rank[nq:]
     meta_out[1] = weight[nq:]
 
-    pl.semaphore_wait(barrier, nq + 2)
-
-    to_sib = [
-        send(meta_out, meta_in, sib_send.at[0], sib_recv.at[0], sibling),
-        send(tok, sib.at[0], sib_send.at[1], sib_recv.at[1], sibling),
-        send(cot, sib.at[1], sib_send.at[2], sib_recv.at[2], sibling),
-    ]
-    for copy in to_sib:
-        copy.start()
-
-    def steps_of(kind, way):
-        return half if (kind + way) % 2 == 0 else half - 1
-
-    def ag_copy(buf, group, kind, way, s):
-        at = buf.at[kind, block_at(-s if way == 0 else s)]
-        return send(at, at, ag_send.at[group, kind, way, s], ag_recv.at[group, kind, way, s], sides[way])
-
-    def ag_start(buf, group):
-        for kind, way in pairs:
-            ag_copy(buf, group, kind, way, 0).start()
-
-    def ag_step(buf, group, s):
-        for kind, way in pairs:
-            ag_copy(buf, group, kind, way, s - 1).wait_recv()
-            if s < steps_of(kind, way):
-                ag_copy(buf, group, kind, way, s).start()
-
-    def ag_last(buf, group):
-        for kind, way in pairs:
-            if steps_of(kind, way) == half:
-                ag_copy(buf, group, kind, way, half - 1).wait_recv()
-
-    def ag_end(buf, group):
-        for kind, way in pairs:
-            for s in range(steps_of(kind, way)):
-                ag_copy(buf, group, kind, way, s).wait_send()
-
-    ag_start(full, 0)
+    to_sib.append(send(meta_out, meta_in, sib_send.at[0], sib_recv.at[0], sibling))
+    to_sib[2].start()
 
     def first_layer(acc, v, g, weights, blk, first):
         gate, up, down = weights
@@ -220,9 +220,9 @@
         blk = block_at(off)
         first_layer(acc_s, full[0, blk], full[1, blk], (sg, su, sd), blk, off == 0)
 
-    def routed_first(off):
+    def routed_first(h, off):
         blk = block_at(off)
-        first_layer(acc_b, b_full[0, blk], b_full[1, blk], (eg, eu, ed), blk, off == 0)
+        first_layer(acc_b.at[h], b_full[h, 0, blk], b_full[h, 1, blk], (eg, eu, ed), blk, off == 0)
 
     shape = (nq, NB, t_rows)
     own_rank = slot_ranks(shape, 0, OWN_ROWS)
@@ -235,6 +235,7 @@
         return pick.reshape(nq * n, t_rows), scaled.reshape(nq * n, t_rows)
 
     own_pick, own_scaled = place(rank[:nq], weight[:nq], own_rank)
+    ag_step(full, 0, 1)
     for copy in to_sib:
         copy.wait_recv()
     sib_pick, sib_scaled = place(meta_in[0], meta_in[1], sib_rank)
@@ -251,13 +252,13 @@
 
         return at
 
-    def start_all(copy):
-        @pl.loop(1, nq)
+    def start_all(copy, first=1, last=nq):
+        @pl.loop(first, last)
         def _(d):
             copy(d).start()
 
-    def wait_all(copy):
-        @pl.loop(1, nq)
+    def wait_all(copy, first=1, last=nq):
+        @pl.loop(first, last)
         def _(d):
             copy(d).wait_recv()
 
@@ -268,6 +269,8 @@
     near_in = swap_copy(4, near_back, near_home, -1)
     b_in = swap_copy(5, ret_send, ret_recv, -1)
 
+    if nx > 1:
+        pl.semaphore_wait(round_sem, nx - 1)
     start_all(b_out)
     b_recv[0] = b_send[0]
 
@@ -290,31 +293,30 @@
         else:
             far_send[:, :, (p - NEAR) * lanes : (p - NEAR + 1) * lanes] = rows
 
-    for load in loads[:3]:
-        load.wait()
-    wide_rows(0)
-    shared_first(0)
-    for s in range(1, half):
+    mid = nq // 2
+
+    def unpack_slabs(ref, h):
+        v = ref[h * mid : (h + 1) * mid].astype(F32)
+        return [v[:, k * NB : (k + 1) * NB].reshape(mid * NB, lanes) for k in range(2)]
+
+    for p in range(NEAR):
+        wide_rows(p)
+    start_all(near_out)
+    near_recv[0] = near_send[0]
+    for s in range(2, half):
         ag_step(full, 0, s)
         for p in (2 * s - 1, 2 * s):
             wide_rows(p)
-        if s == 1:
-            start_all(near_out)
-            near_recv[0] = near_send[0]
-        for p in (2 * s - 1, 2 * s):
-            shared_first(offsets[p])
+
+    for h in range(2):
+        wait_all(b_out, max(1, h * mid), (h + 1) * mid)
+        for kind, v in enumerate(unpack_slabs(b_recv, h)):
+            b_full[h, kind, y] = v.astype(BF16)
+        ag_start(b_full.at[h], 1 + h)
     ag_last(full, 0)
-
-    wait_all(b_out)
-    arrived = b_recv[...].astype(F32)
-    b_full[0, y] = arrived[:, :NB].reshape(nq * NB, lanes).astype(BF16)
-    b_full[1, y] = arrived[:, NB:].reshape(nq * NB, lanes).astype(BF16)
-    ag_start(b_full, 1)
-
     wide_rows(ny - 1)
     start_all(far_out)
     far_recv[0] = far_send[0]
-    shared_first(half)
 
     for k, (pick, scaled) in enumerate(((own_pick, own_scaled), (sib_pick, sib_scaled))):
         high = scaled.astype(BF16).astype(F32)
@@ -346,17 +348,24 @@
 
         return of
 
-    for load in loads[3:]:
+    for load in loads:
         load.wait()
-    routed_first(0)
+    todo = list(offsets)
     for s in range(1, half):
-        ag_step(b_full, 1, s)
-        routed_first(-s)
-        routed_first(s)
+        for h in range(2):
+            ag_step(b_full.at[h], 1 + h, s)
+            for off in ([0] if s == 1 else []) + [-s, s]:
+                routed_first(h, off)
+            share = -(-len(todo) // (2 * (half - s) - h))
+            for off in todo[:share]:
+                shared_first(off)
+            todo = todo[share:]
     shared_mid = middle(acc_s[0], acc_s[1], acc_s[2])
-    ag_last(b_full, 1)
-    routed_first(half)
-    routed_second = second_layer(middle(acc_b[0], acc_b[1], acc_b[2]), (eg, eu, ed))
+
+    def take_wide(p):
+        ref, at = (near_recv, p) if p < NEAR else (far_recv, p - NEAR)
+        v = ref[:, :, at * lanes : (at + 1) * lanes].astype(F32).reshape(nq * NA, lanes).astype(BF16)
+        first_layer(acc_a, v, v, (eg, eu, ed), block_at(offsets[p]), p == 0)
 
     def rs_offset(kind, way, s):
         far = steps_of(kind, way) - s
@@ -397,22 +406,27 @@
             for s in range(steps_of(kind, way)):
                 rs_copy(o, i, group, kind, way, s).wait_send()
 
-    def routed_term(kind, off):
-        return routed_second(kind, block_at(off))
-
-    rs_step(r_out, r_in, 0, 0, routed_term)
+    second_b = []
+
+    def routed_term(h):
+        return lambda kind, off: second_b[h](kind, block_at(off))
+
+    def routed_step(h, s):
+        rs_step(r_out.at[h], r_in.at[h], 1 + h, s, routed_term(h))
+
+    for h in range(2):
+        ag_last(b_full.at[h], 1 + h)
+        routed_first(h, half)
+        second_b.append(second_layer(middle(acc_b[h, 0], acc_b[h, 1], acc_b[h, 2]), (eg, eu, ed)))
+        routed_step(h, 0)
 
     wait_all(near_out)
     for p in range(NEAR):
-        blk = block_at(offsets[p])
-        v = near_recv[:, :, p * lanes : (p + 1) * lanes].astype(F32).reshape(nq * NA, lanes).astype(BF16)
-        first_layer(acc_a, v, v, (eg, eu, ed), blk, p == 0)
+        take_wide(p)
     wait_all(far_out)
     for p in range(NEAR, ny):
-        blk = block_at(offsets[p])
-        v = far_recv[:, :, (p - NEAR) * lanes : (p - NEAR + 1) * lanes]
-        v = v.astype(F32).reshape(nq * NA, lanes).astype(BF16)
-        first_layer(acc_a, v, v, (eg, eu, ed), blk, False)
+        take_wide(p)
+    routed_step(0, 1)
     hid = sg.shape[0]
     slot = lax.broadcasted_iota(jnp.int32, (nq, NA, hid), 1).reshape(nq * NA, hid)
     top_hid = slot < WIDE
@@ -441,18 +455,14 @@
         wide_back(p)
     start_all(far_in)
     far_home[0] = far_back[0]
+    routed_step(1, 1)
     for p in range(NEAR):
         wide_back(p)
     start_all(near_in)
     near_home[0] = near_back[0]
-
-    for s in range(1, half):
-        rs_step(r_out, r_in, 0, s, routed_term)
-    value_b, input_b = rs_total(r_out, r_in, 0, routed_term)
-    slabs = jnp.concatenate((value_b.reshape(nq, NB, lanes), input_b.reshape(nq, NB, lanes)), axis=1)
-    ret_send[...] = slabs.astype(BF16)
-    start_all(b_in)
-    ret_recv[0] = ret_send[0]
+    for s in range(2, half):
+        for h in range(2):
+            routed_step(h, s)
 
     shared_second = second_layer(shared_mid, (sg, su, sd))
 
@@ -466,33 +476,43 @@
             return total + nn_dot(comb_a[1], rows) + nn_dot(comb_a[2], rows)
         return total + nn_dot(comb_a[0], rows)
 
+    def send_home(h):
+        pair = rs_total(r_out.at[h], r_in.at[h], 1 + h, routed_term(h))
+        slabs = jnp.concatenate([v.reshape(mid, NB, lanes) for v in pair], axis=1)
+        ret_send[h * mid : (h + 1) * mid] = slabs.astype(BF16)
+        start_all(b_in, max(1, h * mid), (h + 1) * mid)
+
+    send_home(0)
+    near_from = half - 2
     wait_all(far_in)
-    near_from = half - 2
     for s in range(half):
         if s == near_from:
             wait_all(near_in)
-        rs_step(t_out, t_in, 1, s, token_term)
-    value_t, input_t = rs_total(t_out, t_in, 1, token_term)
+        rs_step(t_out, t_in, 0, s, token_term)
+        if s == 0:
+            send_home(1)
+            ret_recv[0] = ret_send[0]
 
     wait_all(b_in)
-    arrived = ret_recv[...].astype(F32)
-    value_r = arrived[:, :NB].reshape(nq * NB, lanes).astype(BF16)
-    input_r = arrived[:, NB:].reshape(nq * NB, lanes).astype(BF16)
+    halves = [unpack_slabs(ret_recv, h) for h in range(2)]
+    value_r, input_r = (jnp.concatenate([v[k] for v in halves], axis=0).astype(BF16) for k in range(2))
 
     fin_out[0] = nn_dot(comb[1, 1], value_r) + nn_dot(comb[1, 2], value_r)
     fin_out[1] = nn_dot(comb[1, 0], input_r)
     last = send(fin_out, fin_in, sib_send.at[3], sib_recv.at[3], sibling)
     last.start()
+    value_t, input_t = rs_total(t_out, t_in, 0, token_term)
     value_t = value_t + nn_dot(comb[0, 1], value_r) + nn_dot(comb[0, 2], value_r)
     input_t = input_t + nn_dot(comb[0, 0], input_r)
     last.wait_recv()
-    out_v[...] = (value_t + fin_in[0]).astype(BF16)
-    out_i[...] = (input_t + fin_in[1]).astype(BF16)
+    out_v[...] = (value_t + fin_in[0]).astype(out_v.dtype)
+    out_i[...] = (input_t + fin_in[1]).astype(out_i.dtype)
 
     ag_end(full, 0)
-    ag_end(b_full, 1)
-    rs_end(r_out, r_in, 0)
-    rs_end(t_out, t_in, 1)
+    rs_end(t_out, t_in, 0)
+    for h in range(2):
+        ag_end(b_full.at[h], 1 + h)
+        rs_end(r_out.at[h], r_in.at[h], 1 + h)
     for copy in (*to_sib, last):
         copy.wait_send()
 
@@ -529,9 +549,9 @@
             vmem((2, ny, t_rows, lanes), BF16),
             vmem((nq, 2 * NB, lanes), BF16),
             vmem((nq, 2 * NB, lanes), BF16),
-            vmem((2, ny, rows, lanes), BF16),
-            vmem((2, 2, half, rows, lanes), BF16),
-            vmem((2, 2, half, rows, lanes), BF16),
+            vmem((2, 2, ny, rows // 2, lanes), BF16),
+            vmem((2, 2, 2, half, rows // 2, lanes), BF16),
+            vmem((2, 2, 2, half, rows // 2, lanes), BF16),
             vmem((2, 2, half, t_rows, lanes), BF16),
             vmem((2, 2, half, t_rows, lanes), BF16),
             vmem((nq, 2 * NB, lanes), BF16),
@@ -540,19 +560,20 @@
             vmem((2, t_rows, lanes), F32),
             vmem((2, t_rows, lanes), F32),
             vmem((3, t_rows, hid), F32),
-            vmem((3, rows, hid), F32),
+            vmem((2, 3, rows // 2, hid), F32),
             vmem((3, nq * NA, hid), F32),
             vmem((2, 3, t_rows, rows), BF16),
             vmem((3, t_rows, nq * NA), BF16),
             dma((6,)),
             dma((4,)),
             dma((4,)),
-            dma((2, 2, 2, half)),
-            dma((2, 2, 2, half)),
-            dma((2, 2, 2, half)),
-            dma((2, 2, 2, half)),
+            dma((3, 2, 2, half)),
+            dma((3, 2, 2, half)),
+            dma((3, 2, 2, half)),
+            dma((3, 2, 2, half)),
             dma((6, nq)),
             dma((6, nq)),
+            pltpu.SemaphoreType.REGULAR,
         ],
         compiler_params=pltpu.CompilerParams(
             collective_id=0, has_side_effects=True, vmem_limit_bytes=56 * 2**20

time: 109 us -> 101 us (0.927)
  the two profiles are of different devices: /device:TPU:1 before, /device:TPU:6 now
where the time goes in v3:
time: 101 us; the launch traced here: 99.8 us
  Pallas kernels  97 us (96%)
  local copies, waits for them, and re-layouts  2.14 us (2%)
    pallas_call x1, Pallas kernels, on_device(): pl.pallas_call(functools.partial(kernel, (nq, nq // nz, nz, ny)), out_sha...  97 us
    unnamed x4, local copies, waits for them, and re-layouts  2.14 us

profile of v3, /device:TPU:6, one launch (start us, length us, event | category | flops | bytes accessed | tf_op | source)
XLA Modules:
  0.0 99.8 jit_solution(16833283464487369666)
XLA Ops:
  0.6 97.0 %routed_layer.1 = (bf16[128,256]{1,0:T(8,128)(2,1)}, bf16[128,256]{1,0:T(8,128)(2,1)}) custom-call(bf16[128,256]{1,0:T(8,128)(2,1)} %tok.1, bf16[128,256]{1,0:T(8,128)(2,1)} %cot.1, s32[6,128]{1,0:T(8,128)} %bitcast.8, f32[6,128]{1,0:T(8,128)} %bitcast.9, bf16[176,2048]{1,0:T(8,128)(2,1)} %sg_h.1, bf16[176,2048]{1,0:T(8,128)(2,1)} %su_h.1, ...), custom_call_target="tpu_custom_call" | custom-call | tf_op jit(solution)/shard_map/routed_layer/pallas_call | solution.py:539
  97.6 0.0 copy-start
  97.6 1.5 %copy.14 = bf16[128,256]{1,0:T(8,128)(2,1)} copy(bf16[128,256]{1,0:T(8,128)(2,1)} %get-tuple-element.4) | data formatting | bytes 131072
  99.1 0.0 copy-done
  99.1 0.6 copy.15
Async XLA Ops:
  97.6 1.5 %copy-start = (bf16[128,256]{1,0:T(8,128)(2,1)S(1)}, bf16[128,256]{1,0:T(8,128)(2,1)}, u32[]{:S(2)}) copy-start(bf16[128,256]{1,0:T(8,128)(2,1)} %get-tuple-element.5) | copy-start | bytes 196612

commit v4 on v3

--- a/solution.py
+++ b/solution.py
@@ -156,7 +156,7 @@
 
     def ag_copy(buf, group, kind, way, s):
         at = buf.at[kind, block_at(-s if way == 0 else s)]
-        return send(at, at, ag_send.at[group, kind, way, s], ag_recv.at[group, kind, way, s], sides[way])
+        return send(at, at, ag_send.at[group], ag_recv.at[group, kind, way, s], sides[way])
 
     def ag_start(buf, group):
         for kind, way in pairs:
@@ -173,10 +173,8 @@
             if steps_of(kind, way) == half:
                 ag_copy(buf, group, kind, way, half - 1).wait_recv()
 
-    def ag_end(buf, group):
-        for kind, way in pairs:
-            for s in range(steps_of(kind, way)):
-                ag_copy(buf, group, kind, way, s).wait_send()
+    def all_sent(ref, sem):
+        pltpu.make_async_copy(ref, ref, sem).wait()
 
     pl.semaphore_wait(barrier, len(greeted))
     ag_start(full, 0)
@@ -246,32 +244,43 @@
     slabs = jnp.concatenate((x_rows.reshape(nq, NB, lanes), g_rows.reshape(nq, NB, lanes)), axis=1)
     b_send[...] = slabs.astype(BF16)
 
-    def swap_copy(k, src, dst, sign):
-        def at(d):
-            return send(src.at[d], dst.at[d], a2a_send.at[k, d], a2a_recv.at[k, d], at_offset(d, sign))
-
-        return at
-
-    def start_all(copy, first=1, last=nq):
-        @pl.loop(first, last)
-        def _(d):
-            copy(d).start()
-
-    def wait_all(copy, first=1, last=nq):
-        @pl.loop(first, last)
-        def _(d):
-            copy(d).wait_recv()
-
-    b_out = swap_copy(0, b_send, b_recv, 1)
-    near_out = swap_copy(1, near_send, near_recv, 1)
-    far_out = swap_copy(2, far_send, far_recv, 1)
-    far_in = swap_copy(3, far_back, far_home, -1)
-    near_in = swap_copy(4, near_back, near_home, -1)
-    b_in = swap_copy(5, ret_send, ret_recv, -1)
+    mid = nq // 2
+    swaps = []
+
+    class Swap:
+        def __init__(self, src, dst, sign, first=1, last=nq):
+            self.k = len(swaps)
+            self.src, self.dst, self.sign, self.first, self.last = src, dst, sign, first, last
+            swaps.append(self)
+
+        def start(self, first=None, last=None):
+            @pl.loop(self.first if first is None else first, self.last if last is None else last)
+            def _(d):
+                dev = at_offset(d, self.sign)
+                send(self.src.at[d], self.dst.at[d], a2a_send.at[self.k], a2a_recv.at[self.k], dev).start()
+
+        def part(self, ref):
+            return ref.at[pl.ds(self.first, self.last - self.first)]
+
+        def wait(self):
+            all_sent(self.part(self.dst), a2a_recv.at[self.k])
+
+        def end(self):
+            all_sent(self.part(self.src), a2a_send.at[self.k])
+
+    b_out = [Swap(b_send, b_recv, 1, max(1, h * mid), (h + 1) * mid) for h in range(2)]
+    near_out = Swap(near_send, near_recv, 1)
+    far_out = Swap(far_send, far_recv, 1)
+    far_in = Swap(far_back, far_home, -1)
+    near_in = Swap(near_back, near_home, -1)
+    b_in = [Swap(ret_send, ret_recv, -1, max(1, h * mid), (h + 1) * mid) for h in range(2)]
 
     if nx > 1:
         pl.semaphore_wait(round_sem, nx - 1)
-    start_all(b_out)
+    b_out[0].start()
+    if half > 2:
+        ag_step(full, 0, 2)
+    b_out[1].start()
     b_recv[0] = b_send[0]
 
     slot = lax.broadcasted_iota(jnp.int32, (nq, NA, t_rows), 1)
@@ -293,30 +302,161 @@
         else:
             far_send[:, :, (p - NEAR) * lanes : (p - NEAR + 1) * lanes] = rows
 
-    mid = nq // 2
-
     def unpack_slabs(ref, h):
         v = ref[h * mid : (h + 1) * mid].astype(F32)
         return [v[:, k * NB : (k + 1) * NB].reshape(mid * NB, lanes) for k in range(2)]
 
     for p in range(NEAR):
         wide_rows(p)
-    start_all(near_out)
-    near_recv[0] = near_send[0]
-    for s in range(2, half):
+    for s in range(3, half):
         ag_step(full, 0, s)
-        for p in (2 * s - 1, 2 * s):
-            wide_rows(p)
-
     for h in range(2):
-        wait_all(b_out, max(1, h * mid), (h + 1) * mid)
+        b_out[h].wait()
         for kind, v in enumerate(unpack_slabs(b_recv, h)):
             b_full[h, kind, y] = v.astype(BF16)
         ag_start(b_full.at[h], 1 + h)
+        near_out.start(max(1, h * mid), (h + 1) * mid)
+    near_recv[0] = near_send[0]
     ag_last(full, 0)
-    wide_rows(ny - 1)
-    start_all(far_out)
+    for p in range(NEAR, ny):
+        wide_rows(p)
     far_recv[0] = far_send[0]
+
+    def middle(gate, up, grad):
+        act, slope = silu_parts(gate)
+        return (
+            (act * up).astype(BF16),
+            (grad * up * slope).astype(BF16),
+            (grad * act).astype(BF16),
+        )
+
+    def second_layer(mid, weights):
+        hidden, grad_gate, grad_up = mid
+        gate, up, down = weights
+
+        def of(kind, blk):
+            if kind == 0:
+                return nn_dot(hidden, cols(down, blk))
+            return nn_dot(grad_gate, cols(gate, blk)) + nn_dot(grad_up, cols(up, blk))
+
+        return of
+
+    for load in loads:
+        load.wait()
+    def take_wide(p):
+        ref, at = (near_recv, p) if p < NEAR else (far_recv, p - NEAR)
+        v = ref[:, :, at * lanes : (at + 1) * lanes].astype(F32).reshape(nq * NA, lanes).astype(BF16)
+        first_layer(acc_a, v, v, (eg, eu, ed), block_at(offsets[p]), p == 0)
+
+    todo = list(offsets)
+    turns = [(s, h) for s in range(1, half) for h in range(2)]
+    for n, (s, h) in enumerate(turns):
+        ag_step(b_full.at[h], 1 + h, s)
+        if n < 2:
+            far_out.start(max(1, n * mid), (n + 1) * mid)
+        for off in ([0] if s == 1 else []) + [-s, s]:
+            routed_first(h, off)
+        share = -(-len(todo) // (len(turns) - n))
+        for off in todo[:share]:
+            shared_first(off)
+        todo = todo[share:]
+    shared_mid = middle(acc_s[0], acc_s[1], acc_s[2])
+
+    def rs_offset(kind, way, s):
+        far = steps_of(kind, way) - s
+        return far if way == 0 else -far
+
+    def rs_copy(o, i, group, kind, way, s):
+        return send(
+            o.at[kind, way, s],
+            i.at[kind, way, s],
+            rs_send.at[group],
+            rs_recv.at[group, kind, way, s],
+            sides[way],
+        )
+
+    def rs_step(o, i, group, s, compute):
+        for kind, way in pairs:
+            if s < steps_of(kind, way):
+                term = compute(kind, rs_offset(kind, way, s))
+                if s > 0:
+                    rs_copy(o, i, group, kind, way, s - 1).wait_recv()
+                    term = term + i[kind, way, s - 1].astype(F32)
+                o[kind, way, s] = term.astype(BF16)
+                rs_copy(o, i, group, kind, way, s).start()
+
+    def rs_total(o, i, group, compute):
+        totals = []
+        for kind in range(2):
+            total = compute(kind, 0)
+            for way in range(2):
+                n = steps_of(kind, way)
+                rs_copy(o, i, group, kind, way, n - 1).wait_recv()
+                total = total + i[kind, way, n - 1].astype(F32)
+            totals.append(total)
+        return totals
+
+    second_b = []
+
+    def routed_term(h):
+        return lambda kind, off: second_b[h](kind, block_at(off))
+
+    def routed_step(h, s):
+        rs_step(r_out.at[h], r_in.at[h], 1 + h, s, routed_term(h))
+
+    for h in range(2):
+        ag_last(b_full.at[h], 1 + h)
+        routed_first(h, half)
+        second_b.append(second_layer(middle(acc_b[h, 0], acc_b[h, 1], acc_b[h, 2]), (eg, eu, ed)))
+        routed_step(h, 0)
+
+    near_out.wait()
+    for p in range(NEAR):
+        take_wide(p)
+    far_out.wait()
+    for p in range(NEAR, ny):
+        take_wide(p)
+    routed_step(0, 1)
+    hid = sg.shape[0]
+    slot = lax.broadcasted_iota(jnp.int32, (nq, NA, hid), 1).reshape(nq * NA, hid)
+    top_hid = slot < WIDE
+    gate_a, up_a = acc_a[0], acc_a[1]
+    act, slope = silu_parts(gate_a)
+    hidden_a = jnp.where(top_hid, act * up_a, 0.0).astype(BF16)
+
+    def lowered(v):
+        v = v.reshape(nq, NA, hid)
+        return jnp.concatenate((v[:, WIDE:], v[:, :WIDE]), axis=1).reshape(nq * NA, hid)
+
+    grad_a = acc_a[2]
+    grad_gate_a = jnp.where(top_hid, 0.0, grad_a * lowered(up_a) * lowered(slope)).astype(BF16)
+    grad_up_a = jnp.where(top_hid, 0.0, grad_a * lowered(act)).astype(BF16)
+    wide_second = second_layer((hidden_a, grad_gate_a, grad_up_a), (eg, eu, ed))
+
+    def wide_back(p):
+        blk = block_at(offsets[p])
+        rows = (wide_second(0, blk) + wide_second(1, blk)).reshape(nq, NA, lanes).astype(BF16)
+        if p < NEAR:
+            near_back[:, :, p * lanes : (p + 1) * lanes] = rows
+        else:
+            far_back[:, :, (p - NEAR) * lanes : (p - NEAR + 1) * lanes] = rows
+
+    for p in range(NEAR, ny):
+        wide_back(p)
+    far_in.start(1, mid)
+    routed_step(1, 1)
+    far_in.start(mid, nq)
+    far_home[0] = far_back[0]
+    for p in range(NEAR):
+        wide_back(p)
+    near_home[0] = near_back[0]
+    for s in range(2, half):
+        for h in range(2):
+            routed_step(h, s)
+            if s == 2:
+                near_in.start(max(1, h * mid), (h + 1) * mid)
+    if half < 3:
+        near_in.start()
 
     for k, (pick, scaled) in enumerate(((own_pick, own_scaled), (sib_pick, sib_scaled))):
         high = scaled.astype(BF16).astype(F32)
@@ -329,141 +469,6 @@
     comb_a[1] = high.T.astype(BF16)
     comb_a[2] = (wide_scaled - high).T.astype(BF16)
 
-    def middle(gate, up, grad):
-        act, slope = silu_parts(gate)
-        return (
-            (act * up).astype(BF16),
-            (grad * up * slope).astype(BF16),
-            (grad * act).astype(BF16),
-        )
-
-    def second_layer(mid, weights):
-        hidden, grad_gate, grad_up = mid
-        gate, up, down = weights
-
-        def of(kind, blk):
-            if kind == 0:
-                return nn_dot(hidden, cols(down, blk))
-            return nn_dot(grad_gate, cols(gate, blk)) + nn_dot(grad_up, cols(up, blk))
-
-        return of
-
-    for load in loads:
-        load.wait()
-    todo = list(offsets)
-    for s in range(1, half):
-        for h in range(2):
-            ag_step(b_full.at[h], 1 + h, s)
-            for off in ([0] if s == 1 else []) + [-s, s]:
-                routed_first(h, off)
-            share = -(-len(todo) // (2 * (half - s) - h))
-            for off in todo[:share]:
-                shared_first(off)
-            todo = todo[share:]
-    shared_mid = middle(acc_s[0], acc_s[1], acc_s[2])
-
-    def take_wide(p):
-        ref, at = (near_recv, p) if p < NEAR else (far_recv, p - NEAR)
-        v = ref[:, :, at * lanes : (at + 1) * lanes].astype(F32).reshape(nq * NA, lanes).astype(BF16)
-        first_layer(acc_a, v, v, (eg, eu, ed), block_at(offsets[p]), p == 0)
-
-    def rs_offset(kind, way, s):
-        far = steps_of(kind, way) - s
-        return far if way == 0 else -far
-
-    def rs_copy(o, i, group, kind, way, s):
-        return send(
-            o.at[kind, way, s],
-            i.at[kind, way, s],
-            rs_send.at[group, kind, way, s],
-            rs_recv.at[group, kind, way, s],
-            sides[way],
-        )
-
-    def rs_step(o, i, group, s, compute):
-        for kind, way in pairs:
-            if s < steps_of(kind, way):
-                term = compute(kind, rs_offset(kind, way, s))
-                if s > 0:
-                    rs_copy(o, i, group, kind, way, s - 1).wait_recv()
-                    term = term + i[kind, way, s - 1].astype(F32)
-                o[kind, way, s] = term.astype(BF16)
-                rs_copy(o, i, group, kind, way, s).start()
-
-    def rs_total(o, i, group, compute):
-        totals = []
-        for kind in range(2):
-            total = compute(kind, 0)
-            for way in range(2):
-                n = steps_of(kind, way)
-                rs_copy(o, i, group, kind, way, n - 1).wait_recv()
-                total = total + i[kind, way, n - 1].astype(F32)
-            totals.append(total)
-        return totals
-
-    def rs_end(o, i, group):
-        for kind, way in pairs:
-            for s in range(steps_of(kind, way)):
-                rs_copy(o, i, group, kind, way, s).wait_send()
-
-    second_b = []
-
-    def routed_term(h):
-        return lambda kind, off: second_b[h](kind, block_at(off))
-
-    def routed_step(h, s):
-        rs_step(r_out.at[h], r_in.at[h], 1 + h, s, routed_term(h))
-
-    for h in range(2):
-        ag_last(b_full.at[h], 1 + h)
-        routed_first(h, half)
-        second_b.append(second_layer(middle(acc_b[h, 0], acc_b[h, 1], acc_b[h, 2]), (eg, eu, ed)))
-        routed_step(h, 0)
-
-    wait_all(near_out)
-    for p in range(NEAR):
-        take_wide(p)
-    wait_all(far_out)
-    for p in range(NEAR, ny):
-        take_wide(p)
-    routed_step(0, 1)
-    hid = sg.shape[0]
-    slot = lax.broadcasted_iota(jnp.int32, (nq, NA, hid), 1).reshape(nq * NA, hid)
-    top_hid = slot < WIDE
-    gate_a, up_a = acc_a[0], acc_a[1]
-    act, slope = silu_parts(gate_a)
-    hidden_a = jnp.where(top_hid, act * up_a, 0.0).astype(BF16)
-
-    def lowered(v):
-        v = v.reshape(nq, NA, hid)
-        return jnp.concatenate((v[:, WIDE:], v[:, :WIDE]), axis=1).reshape(nq * NA, hid)
-
-    grad_a = acc_a[2]
-    grad_gate_a = jnp.where(top_hid, 0.0, grad_a * lowered(up_a) * lowered(slope)).astype(BF16)
-    grad_up_a = jnp.where(top_hid, 0.0, grad_a * lowered(act)).astype(BF16)
-    wide_second = second_layer((hidden_a, grad_gate_a, grad_up_a), (eg, eu, ed))
-
-    def wide_back(p):
-        blk = block_at(offsets[p])
-        rows = (wide_second(0, blk) + wide_second(1, blk)).reshape(nq, NA, lanes).astype(BF16)
-        if p < NEAR:
-            near_back[:, :, p * lanes : (p + 1) * lanes] = rows
-        else:
-            far_back[:, :, (p - NEAR) * lanes : (p - NEAR + 1) * lanes] = rows
-
-    for p in range(NEAR, ny):
-        wide_back(p)
-    start_all(far_in)
-    far_home[0] = far_back[0]
-    routed_step(1, 1)
-    for p in range(NEAR):
-        wide_back(p)
-    start_all(near_in)
-    near_home[0] = near_back[0]
-    for s in range(2, half):
-        for h in range(2):
-            routed_step(h, s)
-
     shared_second = second_layer(shared_mid, (sg, su, sd))
 
     def token_term(kind, off):
@@ -480,20 +485,21 @@
         pair = rs_total(r_out.at[h], r_in.at[h], 1 + h, routed_term(h))
         slabs = jnp.concatenate([v.reshape(mid, NB, lanes) for v in pair], axis=1)
         ret_send[h * mid : (h + 1) * mid] = slabs.astype(BF16)
-        start_all(b_in, max(1, h * mid), (h + 1) * mid)
+        b_in[h].start()
 
     send_home(0)
     near_from = half - 2
-    wait_all(far_in)
+    far_in.wait()
     for s in range(half):
         if s == near_from:
-            wait_all(near_in)
+            near_in.wait()
         rs_step(t_out, t_in, 0, s, token_term)
         if s == 0:
             send_home(1)
             ret_recv[0] = ret_send[0]
 
-    wait_all(b_in)
+    for swap in b_in:
+        swap.wait()
     halves = [unpack_slabs(ret_recv, h) for h in range(2)]
     value_r, input_r = (jnp.concatenate([v[k] for v in halves], axis=0).astype(BF16) for k in range(2))
 
@@ -508,18 +514,14 @@
     out_v[...] = (value_t + fin_in[0]).astype(out_v.dtype)
     out_i[...] = (input_t + fin_in[1]).astype(out_i.dtype)
 
-    ag_end(full, 0)
-    rs_end(t_out, t_in, 0)
-    for h in range(2):
-        ag_end(b_full.at[h], 1 + h)
-        rs_end(r_out.at[h], r_in.at[h], 1 + h)
+    for group, buf in enumerate((full, b_full.at[0], b_full.at[1])):
+        sent = buf.at[:, pl.ds(0, ny - 1)]
+        all_sent(sent, ag_send.at[group])
+        all_sent(sent, rs_send.at[group])
     for copy in (*to_sib, last):
         copy.wait_send()
-
-    @pl.loop(1, nq)
-    def _(d):
-        for copy in (b_out, near_out, far_out, far_in, near_in, b_in):
-            copy(d).wait_send()
+    for swap in swaps:
+        swap.end()
 
 
 def on_device(*args):
@@ -567,12 +569,12 @@
             dma((6,)),
             dma((4,)),
             dma((4,)),
+            dma((3,)),
             dma((3, 2, 2, half)),
+            dma((3,)),
             dma((3, 2, 2, half)),
-            dma((3, 2, 2, half)),
-            dma((3, 2, 2, half)),
-            dma((6, nq)),
-            dma((6, nq)),
+            dma((8,)),
+            dma((8,)),
             pltpu.SemaphoreType.REGULAR,
         ],
         compiler_params=pltpu.CompilerParams(

time: 101 us -> 96 us (0.950)
  Pallas kernels: 97 us -> 91.3 us
    pallas_call x1, Pallas kernels: 97 us -> 91.3 us  [on_device(): pl.pallas_call(functools.partial(kernel, (nq, nq // nz, nz, ny)), out_sha...]
where the time goes in v4:
time: 96 us; the launch traced here: 94.1 us
  Pallas kernels  91.3 us (95%)
  local copies, waits for them, and re-layouts  2.14 us (2%)
    pallas_call x1, Pallas kernels, on_device(): pl.pallas_call(functools.partial(kernel, (nq, nq // nz, nz, ny)), out_sha...  91.3 us
    unnamed x4, local copies, waits for them, and re-layouts  2.14 us

profile of v4, /device:TPU:6, one launch (start us, length us, event | category | flops | bytes accessed | tf_op | source)
XLA Modules:
  0.0 94.1 jit_solution(8686100994865933706)
XLA Ops:
  0.6 91.3 %routed_layer.1 = (bf16[128,256]{1,0:T(8,128)(2,1)}, bf16[128,256]{1,0:T(8,128)(2,1)}) custom-call(bf16[128,256]{1,0:T(8,128)(2,1)} %tok.1, bf16[128,256]{1,0:T(8,128)(2,1)} %cot.1, s32[6,128]{1,0:T(8,128)} %bitcast.8, f32[6,128]{1,0:T(8,128)} %bitcast.9, bf16[176,2048]{1,0:T(8,128)(2,1)} %sg_h.1, bf16[176,2048]{1,0:T(8,128)(2,1)} %su_h.1, ...), custom_call_target="tpu_custom_call" | custom-call | tf_op jit(solution)/shard_map/routed_layer/pallas_call | solution.py:541
  92.0 0.0 copy-start
  92.0 1.5 %copy.14 = bf16[128,256]{1,0:T(8,128)(2,1)} copy(bf16[128,256]{1,0:T(8,128)(2,1)} %get-tuple-element.4) | data formatting | bytes 131072
  93.5 0.0 copy-done
  93.5 0.6 copy.15
Async XLA Ops:
  92.0 1.5 %copy-start = (bf16[128,256]{1,0:T(8,128)(2,1)S(1)}, bf16[128,256]{1,0:T(8,128)(2,1)}, u32[]{:S(2)}) copy-start(bf16[128,256]{1,0:T(8,128)(2,1)} %get-tuple-element.5) | copy-start | bytes 196612

commit v5 on v4

--- a/solution.py
+++ b/solution.py
@@ -308,19 +308,21 @@
 
     for p in range(NEAR):
         wide_rows(p)
+    near_out.start(1, mid)
     for s in range(3, half):
         ag_step(full, 0, s)
+    near_out.start(mid, nq)
     for h in range(2):
         b_out[h].wait()
         for kind, v in enumerate(unpack_slabs(b_recv, h)):
             b_full[h, kind, y] = v.astype(BF16)
         ag_start(b_full.at[h], 1 + h)
-        near_out.start(max(1, h * mid), (h + 1) * mid)
     near_recv[0] = near_send[0]
     ag_last(full, 0)
     for p in range(NEAR, ny):
         wide_rows(p)
     far_recv[0] = far_send[0]
+    far_out.start(1, mid)
 
     def middle(gate, up, grad):
         act, slope = silu_parts(gate)
@@ -352,8 +354,12 @@
     turns = [(s, h) for s in range(1, half) for h in range(2)]
     for n, (s, h) in enumerate(turns):
         ag_step(b_full.at[h], 1 + h, s)
-        if n < 2:
-            far_out.start(max(1, n * mid), (n + 1) * mid)
+        if n == 1:
+            far_out.start(mid, nq)
+        if n == len(turns) - 1:
+            near_out.wait()
+            for p in range(NEAR):
+                take_wide(p)
         for off in ([0] if s == 1 else []) + [-s, s]:
             routed_first(h, off)
         share = -(-len(todo) // (len(turns) - n))
@@ -386,14 +392,11 @@
                 rs_copy(o, i, group, kind, way, s).start()
 
     def rs_total(o, i, group, compute):
-        totals = []
-        for kind in range(2):
-            total = compute(kind, 0)
-            for way in range(2):
-                n = steps_of(kind, way)
-                rs_copy(o, i, group, kind, way, n - 1).wait_recv()
-                total = total + i[kind, way, n - 1].astype(F32)
-            totals.append(total)
+        totals = [compute(kind, 0) for kind in range(2)]
+        for kind, way in pairs:
+            n = steps_of(kind, way)
+            rs_copy(o, i, group, kind, way, n - 1).wait_recv()
+            totals[kind] = totals[kind] + i[kind, way, n - 1].astype(F32)
         return totals
 
     second_b = []
@@ -410,13 +413,9 @@
         second_b.append(second_layer(middle(acc_b[h, 0], acc_b[h, 1], acc_b[h, 2]), (eg, eu, ed)))
         routed_step(h, 0)
 
-    near_out.wait()
-    for p in range(NEAR):
-        take_wide(p)
     far_out.wait()
     for p in range(NEAR, ny):
         take_wide(p)
-    routed_step(0, 1)
     hid = sg.shape[0]
     slot = lax.broadcasted_iota(jnp.int32, (nq, NA, hid), 1).reshape(nq * NA, hid)
     top_hid = slot < WIDE
@@ -444,9 +443,10 @@
     for p in range(NEAR, ny):
         wide_back(p)
     far_in.start(1, mid)
-    routed_step(1, 1)
+    routed_step(0, 1)
     far_in.start(mid, nq)
     far_home[0] = far_back[0]
+    routed_step(1, 1)
     for p in range(NEAR):
         wide_back(p)
     near_home[0] = near_back[0]

time: 96 us -> 93.1 us (0.970)
  Pallas kernels: 91.3 us -> 89.2 us
    pallas_call x1, Pallas kernels: 91.3 us -> 89.2 us  [on_device(): pl.pallas_call(functools.partial(kernel, (nq, nq // nz, nz, ny)), out_sha...]
where the time goes in v5:
time: 93.1 us; the launch traced here: 92 us
  Pallas kernels  89.2 us (96%)
  local copies, waits for them, and re-layouts  2.14 us (2%)
    pallas_call x1, Pallas kernels, on_device(): pl.pallas_call(functools.partial(kernel, (nq, nq // nz, nz, ny)), out_sha...  89.2 us
    unnamed x4, local copies, waits for them, and re-layouts  2.14 us

profile of v5, /device:TPU:6, one launch (start us, length us, event | category | flops | bytes accessed | tf_op | source)
XLA Modules:
  0.0 92.0 jit_solution(6064698912150566388)
XLA Ops:
  0.6 89.2 %routed_layer.1 = (bf16[128,256]{1,0:T(8,128)(2,1)}, bf16[128,256]{1,0:T(8,128)(2,1)}) custom-call(bf16[128,256]{1,0:T(8,128)(2,1)} %tok.1, bf16[128,256]{1,0:T(8,128)(2,1)} %cot.1, s32[6,128]{1,0:T(8,128)} %bitcast.8, f32[6,128]{1,0:T(8,128)} %bitcast.9, bf16[176,2048]{1,0:T(8,128)(2,1)} %sg_h.1, bf16[176,2048]{1,0:T(8,128)(2,1)} %su_h.1, ...), custom_call_target="tpu_custom_call" | custom-call | tf_op jit(solution)/shard_map/routed_layer/pallas_call | solution.py:541
  89.8 0.0 copy-start
  89.8 1.5 %copy.14 = bf16[128,256]{1,0:T(8,128)(2,1)} copy(bf16[128,256]{1,0:T(8,128)(2,1)} %get-tuple-element.4) | data formatting | bytes 131072
  91.3 0.0 copy-done
  91.3 0.6 copy.15
Async XLA Ops:
  89.8 1.5 %copy-start = (bf16[128,256]{1,0:T(8,128)(2,1)S(1)}, bf16[128,256]{1,0:T(8,128)(2,1)}, u32[]{:S(2)}) copy-start(bf16[128,256]{1,0:T(8,128)(2,1)} %get-tuple-element.5) | copy-start | bytes 196612

commit v6 on v5

--- a/solution.py
+++ b/solution.py
@@ -51,8 +51,7 @@
     eg_h,
     eu_h,
     ed_h,
-    out_v,
-    out_i,
+    out,
     sg,
     su,
     sd,
@@ -511,8 +510,8 @@
     value_t = value_t + nn_dot(comb[0, 1], value_r) + nn_dot(comb[0, 2], value_r)
     input_t = input_t + nn_dot(comb[0, 0], input_r)
     last.wait_recv()
-    out_v[...] = (value_t + fin_in[0]).astype(out_v.dtype)
-    out_i[...] = (input_t + fin_in[1]).astype(out_i.dtype)
+    out[0] = (value_t + fin_in[0]).astype(out.dtype)
+    out[1] = (input_t + fin_in[1]).astype(out.dtype)
 
     for group, buf in enumerate((full, b_full.at[0], b_full.at[1])):
         sent = buf.at[:, pl.ds(0, ny - 1)]
@@ -535,14 +534,13 @@
     eg, eu, ed = (w.reshape(hid, feats) for w in (eg, eu, ed))
     rows = nq * NB
     vmem, dma = pltpu.VMEM, pltpu.SemaphoreType.DMA
-    out = jax.ShapeDtypeStruct((t_rows, lanes), BF16)
     in_vmem = pl.BlockSpec(memory_space=pltpu.VMEM)
     in_any = pl.BlockSpec(memory_space=pl.ANY)
-    return pl.pallas_call(
+    both = pl.pallas_call(
         functools.partial(kernel, (nq, nq // nz, nz, ny)),
-        out_shape=(out, out),
+        out_shape=jax.ShapeDtypeStruct((2, t_rows, lanes), BF16),
         in_specs=[in_vmem] * 4 + [in_any] * 6,
-        out_specs=(in_vmem, in_vmem),
+        out_specs=in_vmem,
         scratch_shapes=[
             *[vmem((hid, feats), BF16)] * 6,
             vmem((2, nq, t_rows), F32),
@@ -582,6 +580,7 @@
         ),
         name="routed_layer",
     )(tokens, cotangent, route_ids.T, route_weights.T, sg, su, sd, eg, eu, ed)
+    return both[0], both[1]
 
 
 def solution(mesh):

time: 93.1 us -> 92.6 us (level)
    unnamed x4 -> x0, local copies, waits for them, and re-layouts: 2.14 us -> none
    squeeze x0 -> x1, local copies, waits for them, and re-layouts: none -> 1.53 us  [on_device(): return (both[0], both[1])]
where the time goes in v6:
time: 92.6 us; the launch traced here: 91.4 us
  Pallas kernels  89.2 us (96%)
  local copies, waits for them, and re-layouts  1.53 us (2%)
    pallas_call x1, Pallas kernels, on_device(): pl.pallas_call(functools.partial(kernel, (nq, nq // nz, nz, ny)), out_sha...  89.2 us

profile of v6, /device:TPU:6, one launch (start us, length us, event | category | flops | bytes accessed | tf_op | source)
XLA Modules:
  0.0 91.4 jit_solution(15935634691067301102)
XLA Ops:
  0.6 89.2 %routed_layer.1 = bf16[2,128,256]{2,1,0:T(8,128)(2,1)} custom-call(bf16[128,256]{1,0:T(8,128)(2,1)} %tok.1, bf16[128,256]{1,0:T(8,128)(2,1)} %cot.1, s32[6,128]{1,0:T(8,128)} %bitcast.12, f32[6,128]{1,0:T(8,128)} %bitcast.13, bf16[176,2048]{1,0:T(8,128)(2,1)} %sg_h.1, bf16[176,2048]{1,0:T(8,128)(2,1)} %su_h.1, bf16[176,2048]{1,0:T(8,128)(2,1)} %sd_h.1, ...), custom_call_target="tpu_custom_call" | custom-call | tf_op jit(solution)/shard_map/routed_layer/pallas_call | solution.py:539
  89.9 1.5 %slice_bitcast_fusion = (bf16[128,256]{1,0:T(8,128)(2,1)}, bf16[128,256]{1,0:T(8,128)(2,1)}) fusion(bf16[2,128,256]{2,1,0:T(8,128)(2,1)} %routed_layer.1), kind=kLoop, calls=%fused_computation | loop fusion | bytes 262144 | tf_op jit(solution)/shard_map/squeeze | solution.py:583
